TPU v7x, 32 devices: a whole 2x2x4 slice. The times are simulated.
32 devices in a mesh: row: 8 (over y, x, core), col: 4 (over z).
Axes of the slice: x: 2, y: 2, z: 4, core: 2. Of those that a mesh axis runs over, the one named last changes fastest.
Arguments:
- field_in: bfloat16 [256, 256, 256], P('row', 'col'), may hold values from -40 to 40
- cotangent: bfloat16 [256, 256, 256], P('row', 'col'), may hold values from -6 to 6
- gain_conv: float32 [256], replicated, may hold values from 0.1 to 1.9
- w_expand: bfloat16 [256, 1024], replicated, may hold values from -0.375 to 0.375
- w_depth: float32 [3, 3, 1024], replicated, may hold values from -4 to 4
- w_project: bfloat16 [1024, 256], replicated, may hold values from -0.1875 to 0.1875
- gain_attn: float32 [256], replicated, may hold values from 0.1 to 1.9
- w_qkv: bfloat16 [256, 768], replicated, may hold values from -1.25 to 1.25
- w_out: bfloat16 [256, 256], replicated, may hold values from -0.375 to 0.375
Outputs:
- grad_field: bfloat16 [256, 256, 256], P('row', 'col')
- grad_gain_conv: float32 [256], replicated
- grad_expand: float32 [256, 1024], replicated
- grad_depth: float32 [3, 3, 1024], replicated
- grad_project: float32 [1024, 256], replicated
- grad_gain_attn: float32 [256], replicated
- grad_qkv: float32 [256, 768], replicated
- grad_out: float32 [256, 256], replicated
All inputs are finite; a program needn't handle non-finite values.
Results may differ from a plain program's by a relative error of at most 0.025.
The roundings to bfloat16 on the way count: a program that leaves them out, or rounds other values in their place, can miss the bound.
Values may be sent and summed in bfloat16 or wider, within the bound.
A program may use at most 192 MiB of HBM per device.

v0:
```python
import jax
import jax.numpy as jnp
from jax import lax
from jax.sharding import PartitionSpec as P

HEADS = 8
GRID = 16


norm_eps = 1e-05
root_half = 0.7071067811865476
inv_root_two_pi = 0.3989422804014327


def padded_2(block, sides, width):
    for axis, dim in sides:
        count = lax.axis_size(axis)
        forward = [(i, i + 1) for i in range(count - 1)]
        backward = [(target, source) for source, target in forward]
        low = lax.ppermute(
            lax.slice_in_dim(block, block.shape[dim] - width, None, axis=dim), axis, forward
        )
        high = lax.ppermute(lax.slice_in_dim(block, 0, width, axis=dim), axis, backward)
        block = jnp.concatenate([low, block, high], axis=dim)
    return block


def gelu_value(values):
    return 0.5 * values * (1.0 + lax.erf(values * root_half))


def gelu_slope(values):
    return (
        0.5 * (1.0 + lax.erf(values * root_half))
        + values * jnp.exp(-0.5 * values * values) * inv_root_two_pi
    )


def normalize(values):
    centre = jnp.mean(values, axis=-1, keepdims=True)
    centred = values - centre
    inv_dev = lax.rsqrt(jnp.mean(centred * centred, axis=-1, keepdims=True) + norm_eps)
    return (centred * inv_dev, inv_dev)


def normalize_back(grad_normed, normed, inv_dev):
    return inv_dev * (
        grad_normed
        - jnp.mean(grad_normed, axis=-1, keepdims=True)
        - normed * jnp.mean(grad_normed * normed, axis=-1, keepdims=True)
    )


def product(form, left, right):
    return jnp.einsum(form, left, right, preferred_element_type=jnp.float32)


def expand_rows(block_in, gain_conv, w_expand):
    flat_rows = block_in.reshape(-1, block_in.shape[-1]).astype(jnp.float32)
    normed, inv_dev = normalize(flat_rows)
    scaled = (normed * gain_conv).astype(jnp.bfloat16)
    pre_act = jnp.dot(scaled, w_expand, preferred_element_type=jnp.float32)
    return (normed, inv_dev, scaled, pre_act)


def depthwise(padded, w_depth, row_count, col_count):
    summed = jnp.zeros((row_count, col_count, padded.shape[-1]), jnp.float32)
    for row_off in range(3):
        for col_off in range(3):
            summed = (
                summed
                + padded[row_off : row_off + row_count, col_off : col_off + col_count].astype(
                    jnp.float32
                )
                * w_depth[row_off, col_off]
            )
    return summed


def spread_back(grad_pad, w_depth, row_count, col_count):
    summed = jnp.zeros((row_count, col_count, grad_pad.shape[-1]), jnp.float32)
    for row_off in range(3):
        for col_off in range(3):
            summed = (
                summed
                + grad_pad[
                    2 - row_off : 2 - row_off + row_count, 2 - col_off : 2 - col_off + col_count
                ].astype(jnp.float32)
                * w_depth[row_off, col_off]
            )
    return summed


def depth_grad(hidden_pad, grad_conv, row_count, col_count):
    grad_wide = grad_conv.astype(jnp.float32)
    pieces = []
    for row_off in range(3):
        for col_off in range(3):
            pieces.append(
                jnp.sum(
                    hidden_pad[row_off : row_off + row_count, col_off : col_off + col_count].astype(
                        jnp.float32
                    )
                    * grad_wide,
                    axis=(0, 1),
                )
            )
    return jnp.stack(pieces).reshape(3, 3, -1)


def window_back(windows, cot_windows, gain_attn, w_qkv, w_out):
    count, length, chans = windows.shape
    head_size = chans // HEADS
    scale_qk = head_size ** (-0.5)
    normed, inv_dev = normalize(windows.astype(jnp.float32))
    scaled = (normed * gain_attn).astype(jnp.bfloat16)
    projected = product("wtc,cd->wtd", scaled, w_qkv).astype(jnp.bfloat16)
    query = projected[..., :chans].reshape(count, length, HEADS, head_size)
    keys_all = projected[..., chans : 2 * chans].reshape(count, length, HEADS, head_size)
    values_all = projected[..., 2 * chans :].reshape(count, length, HEADS, head_size)
    scores = product("wqhd,wkhd->whqk", query, keys_all) * scale_qk
    scores = scores - jnp.max(scores, axis=-1, keepdims=True)
    expons = jnp.exp(scores)
    probs = expons / jnp.sum(expons, axis=-1, keepdims=True)
    probs_b = probs.astype(jnp.bfloat16)
    attended = (
        product("whqk,wkhd->wqhd", probs_b, values_all)
        .astype(jnp.bfloat16)
        .reshape(count, length, chans)
    )
    grad_att = (
        product("wtd,cd->wtc", cot_windows, w_out)
        .astype(jnp.bfloat16)
        .reshape(count, length, HEADS, head_size)
    )
    grad_out = product("wtc,wtd->cd", attended, cot_windows)
    grad_probs = product("wqhd,wkhd->whqk", grad_att, values_all)
    grad_value = product("whqk,wqhd->wkhd", probs_b, grad_att).astype(jnp.bfloat16)
    grad_scores = (
        scale_qk * probs * (grad_probs - jnp.sum(grad_probs * probs, axis=-1, keepdims=True))
    ).astype(jnp.bfloat16)
    grad_query = product("whqk,wkhd->wqhd", grad_scores, keys_all).astype(jnp.bfloat16)
    grad_key = product("whqk,wqhd->wkhd", grad_scores, query).astype(jnp.bfloat16)
    grad_proj = jnp.concatenate(
        [
            grad_query.reshape(count, length, chans),
            grad_key.reshape(count, length, chans),
            grad_value.reshape(count, length, chans),
        ],
        axis=-1,
    )
    grad_qkv = product("wtc,wtd->cd", scaled, grad_proj)
    grad_scaled = product("wtd,cd->wtc", grad_proj, w_qkv)
    grad_gain = jnp.sum(grad_scaled * normed, axis=(0, 1))
    grad_branch = normalize_back(grad_scaled * gain_attn, normed, inv_dev).astype(jnp.bfloat16)
    return (grad_branch, (grad_qkv, grad_out, grad_gain))


def shards(field_in, cotangent, gain_conv, w_expand, w_depth, w_project, gain_attn, w_qkv, w_out):
    rows_dev, cols_dev, chans = field_in.shape
    expand_w = w_expand.shape[1]
    row_devices = lax.axis_size("row")
    col_devices = lax.axis_size("col")
    grad_scale = (rows_dev * cols_dev * row_devices * col_devices) ** (-0.5)
    normed, inv_dev, scaled, pre_act = expand_rows(field_in, gain_conv, w_expand)
    hidden = gelu_value(pre_act).astype(jnp.bfloat16).reshape(rows_dev, cols_dev, expand_w)
    hidden_pad = padded_2(hidden, (("row", 0), ("col", 1)), 1)
    conv = depthwise(hidden_pad, w_depth, rows_dev, cols_dev).reshape(-1, expand_w)
    acted = gelu_value(conv).astype(jnp.bfloat16)
    mid_flat = field_in.reshape(-1, chans).astype(jnp.float32) + jnp.dot(
        acted, w_project, preferred_element_type=jnp.float32
    )
    mid_tile = mid_flat.astype(jnp.bfloat16).reshape(rows_dev, cols_dev, chans)
    grid_per_row = GRID // row_devices
    grid_per_col = GRID // col_devices
    span_rows = rows_dev // grid_per_row
    span_cols = cols_dev // grid_per_col
    part_rows = span_rows // row_devices
    part_cols = span_cols // col_devices
    window_count = part_rows * part_cols
    stacked = jnp.stack([mid_tile, cotangent])
    arranged = stacked.reshape(
        2, grid_per_row, row_devices, part_rows, grid_per_col, col_devices, part_cols, chans
    )
    arranged = arranged.transpose(0, 2, 5, 1, 4, 3, 6, 7).reshape(
        2, row_devices * col_devices, grid_per_row, grid_per_col, part_rows, part_cols, chans
    )
    moved = lax.all_to_all(arranged, ("row", "col"), split_axis=1, concat_axis=1, tiled=True)
    moved = moved.reshape(
        2, row_devices, col_devices, grid_per_row, grid_per_col, part_rows, part_cols, chans
    )
    paired = moved.transpose(0, 5, 6, 1, 3, 2, 4, 7)
    group = 4
    paired = paired.reshape(2, window_count // group, group, GRID * GRID, chans)

    def attend_step(carry, window_pair):
        grad_branch, sums = window_back(window_pair[0], window_pair[1], gain_attn, w_qkv, w_out)
        return (tuple((before + added for before, added in zip(carry, sums))), grad_branch)

    attn_init = (
        jnp.zeros((chans, 3 * chans), jnp.float32),
        jnp.zeros((chans, chans), jnp.float32),
        jnp.zeros((chans,), jnp.float32),
    )
    attn_sums, grad_windows = lax.scan(attend_step, attn_init, (paired[0], paired[1]))
    grad_qkv_part, grad_out_part, grad_gain_part = attn_sums
    arranged = grad_windows.reshape(
        part_rows, part_cols, row_devices, grid_per_row, col_devices, grid_per_col, chans
    )
    arranged = arranged.transpose(2, 4, 3, 5, 0, 1, 6).reshape(
        row_devices * col_devices, grid_per_row, grid_per_col, part_rows, part_cols, chans
    )
    moved = lax.all_to_all(arranged, ("row", "col"), split_axis=0, concat_axis=0, tiled=True)
    moved = moved.reshape(
        row_devices, col_devices, grid_per_row, grid_per_col, part_rows, part_cols, chans
    )
    grad_tile = moved.transpose(2, 0, 4, 3, 1, 5, 6).reshape(rows_dev, cols_dev, chans)
    grad_mid = cotangent.reshape(-1, chans).astype(jnp.float32) + grad_tile.reshape(
        -1, chans
    ).astype(jnp.float32)
    grad_mid_b = grad_mid.astype(jnp.bfloat16)
    grad_project = jnp.dot(acted.T, grad_mid_b, preferred_element_type=jnp.float32)
    grad_acted = jnp.dot(grad_mid_b, w_project.T, preferred_element_type=jnp.float32).astype(
        jnp.bfloat16
    )
    grad_conv = (
        (grad_acted.astype(jnp.float32) * gelu_slope(conv))
        .astype(jnp.bfloat16)
        .reshape(rows_dev, cols_dev, expand_w)
    )
    grad_pad = padded_2(grad_conv, (("row", 0), ("col", 1)), 1)
    grad_depth = depth_grad(hidden_pad, grad_conv, rows_dev, cols_dev)
    grad_hidden = spread_back(grad_pad, w_depth, rows_dev, cols_dev).reshape(-1, expand_w)
    grad_pre = (grad_hidden * gelu_slope(pre_act)).astype(jnp.bfloat16)
    grad_expand = jnp.dot(scaled.T, grad_pre, preferred_element_type=jnp.float32)
    grad_scaled = jnp.dot(grad_pre, w_expand.T, preferred_element_type=jnp.float32)
    grad_gain_conv = jnp.sum(grad_scaled * normed, axis=0)
    grad_field = (
        (grad_mid + normalize_back(grad_scaled * gain_conv, normed, inv_dev))
        .astype(jnp.bfloat16)
        .reshape(rows_dev, cols_dev, chans)
    )
    (
        grad_gain_conv,
        grad_expand,
        grad_depth,
        grad_project,
        grad_gain_part,
        grad_qkv_part,
        grad_out_part,
    ) = lax.psum(
        (
            grad_gain_conv,
            grad_expand,
            grad_depth,
            grad_project,
            grad_gain_part,
            grad_qkv_part,
            grad_out_part,
        ),
        ("row", "col"),
    )
    return (
        grad_field,
        grad_gain_conv * grad_scale,
        grad_expand * grad_scale,
        grad_depth * grad_scale,
        grad_project * grad_scale,
        grad_gain_part * grad_scale,
        grad_qkv_part * grad_scale,
        grad_out_part * grad_scale,
    )


def solution(mesh):
    in_specs = (P("row", "col", None), P("row", "col", None), P(), P(), P(), P(), P(), P(), P())
    out_specs = (P("row", "col", None), P(), P(), P(), P(), P(), P(), P())
    return jax.shard_map(shards, mesh=mesh, in_specs=in_specs, out_specs=out_specs, check_vma=False)
```

profile of v0, /device:TPU:0, one launch (start us, length us, event | category | flops | bytes accessed | tf_op | source)
XLA Modules:
  0.0 475.2 jit_solution(9517938279580190930)
XLA Ops:
  13.3 4.6 multiply_convert_fusion.2
  21.6 4.0 collective-permute-done.1
  25.8 3.5 collective-permute-start.2
  31.9 4.4 collective-permute-done.3
  36.3 5.7 %maximum_maximum_fusion = (bf16[34,65,1024]{2,1,0:T(8,128)(2,1)S(1)}, bf16[34,65,1024]{2,1,0:T(8,128)(2,1)S(1)}) fusion(bf16[1,64,1024]{2,1,0:T(8,128)(2,1)S(1)} %collective-permute-done.1, bf16[32,64,1024]{2,1,0:T(8,128)(2,1)} %bitcast.249, bf16[1,64,1024]{2,1,0:T(8,128)(2,1)S(1)} %collective-permute-done, ...), kind=kLoop, calls=%fused_computation.120 | loop fusion | flops 36208640 | bytes 13647872 | tf_op jit(solution)/shard_map/concatenate | solution.py:24
  42.1 12.1 %fusion.50 = f32[32,64,1024]{2,1,0:T(8,128)S(1)} fusion(bf16[32,64,1024]{2,1,0:T(8,128)(2,1)S(1)} %bitcast.251, bf16[1,64,1024]{2,1,0:T(8,128)(2,1)S(1)} %collective-permute-done.1, bf16[1,64,1024]{2,1,0:T(8,128)(2,1)S(1)} %collective-permute-done, f32[1024]{0:T(1024)S(1)} %bitcast.290, f32[1024]{0:T(1024)S(1)} %bitcast.292, f32[1024]{0:T(1024)S(1)} %bitcast.278, ...), kind=kLoop, calls=%fused_computation.84 | loop fusion | flops 58720256 | bytes 38047744 | tf_op jit(solution)/shard_map/add | solution.py:71
  54.2 6.0 %fusion.77 = (bf16[2048,1024]{1,0:T(8,128)(2,1)S(1)}, f32[2048,1024]{1,0:T(8,128)}) fusion(f32[32,64,1024]{2,1,0:T(8,128)S(1)} %fusion.50), kind=kLoop, calls=%fused_computation.113 | loop fusion | flops 10485760 | bytes 20971520 | tf_op jit(solution)/shard_map/convert_element_type | solution.py:169
  66.5 2.5 copy.84
  69.0 7.7 %all-to-all-start = ((bf16[2,32,2,4,2,4,256]{6,5,4,3,2,0,1:T(4,128)(2,1)}), bf16[2,32,2,4,2,4,256]{6,5,4,3,2,0,1:T(4,128)(2,1)S(1)}, u32[]{:S(2)}, u32[]{:S(2)}) async-start(bf16[2,32,2,4,2,4,256]{6,5,4,3,2,0,1:T(4,128)(2,1)} %copy.84), calls=%async_computation | async-start | bytes 4194304 | tf_op jit(solution)/shard_map/all_to_all | solution.py:188
  77.0 47.3 %all-to-all-done = bf16[2,32,2,4,2,4,256]{6,5,4,3,2,0,1:T(4,128)(2,1)S(1)} async-done(((bf16[2,32,2,4,2,4,256]{6,5,4,3,2,0,1:T(4,128)(2,1)}), bf16[2,32,2,4,2,4,256]{6,5,4,3,2,0,1:T(4,128)(2,1)S(1)}, u32[]{:S(2)}, u32[]{:S(2)}) %all-to-all-start) | async-done | bytes 2097184 | tf_op jit(solution)/shard_map/all_to_all | solution.py:188
  130.1 83.4 %while.17 = (s32[]{:T(128)}, f32[256,768]{1,0:T(8,128)}, f32[256,256]{1,0:T(8,128)S(1)}, f32[256]{0:T(256)S(1)}, bf16[2,4,256,256]{3,1,2,0:T(4,128)(2,1)}, /*ind...) while((s32[]{:T(128)}, f32[256,768]{1,0:T(8,128)}, ...), condition=%wide.region_11.12_spmd.clone, body=%wide.region_2.11_spmd.clone.sunk | while | flops 2334123520 | bytes 148312384 | solution.py:205
  138.5 5.6 %fusion.163 = (f32[4,8,256]{2,1,0:T(8,128)}, f32[4,8,256,256]{2,3,1,0:T(8,128)}) fusion(bf16[4,256,8,32]{1,3,2,0:T(8,128)(2,1)S(1)} %bitcast.260, bf16[4,256,8,32]{1,3,2,0:T(8,128)(2,1)S(1)} %bitcast.252), kind=kOutput, calls=%fused_computation.172.clone.1 | convolution fusion | flops 140509440 | bytes 9469952 | tf_op jit(solution)/shard_map/while/body/eval_jaxpr/sub | solution.py:122
  144.2 4.4 fusion.166
  154.4 4.8 %multiply_reduce_fusion.9 = (f32[4,8,256]{2,1,0:T(8,128)S(1)}, f32[4,8,256,256]{2,3,1,0:T(8,128)S(1)}) fusion(f32[4,8,256,256]{2,3,1,0:T(8,128)} %get-tuple-element.297, f32[4,8,256]{2,1,0:T(8,128)} %get-tuple-element.298, bf16[4,256,8,32]{1,3,2,0:T(8,128)(2,1)S(1)} %bitcast.265, bf16[4,256,8,32]{1,3,2,0:T(8,128)(2,1)S(1)} %bitcast.267), kind=kOutput, calls=%fused_computation.2.clone.1 | convolution fusion | flops 140500992 | bytes 17891328 | tf_op jit(solution)/shard_map/while/body/eval_jaxpr/wqhd,wkhd->whqk/dot_general | solution.py:55
  159.2 4.4 multiply_convert_fusion.8
  179.6 5.6 %fusion.163 = (f32[4,8,256]{2,1,0:T(8,128)}, f32[4,8,256,256]{2,3,1,0:T(8,128)}) fusion(bf16[4,256,8,32]{1,3,2,0:T(8,128)(2,1)S(1)} %bitcast.260, bf16[4,256,8,32]{1,3,2,0:T(8,128)(2,1)S(1)} %bitcast.252), kind=kOutput, calls=%fused_computation.172.clone.1 | convolution fusion | flops 140509440 | bytes 9469952 | tf_op jit(solution)/shard_map/while/body/eval_jaxpr/sub | solution.py:122
  185.3 4.4 fusion.166
  195.5 4.8 %multiply_reduce_fusion.9 = (f32[4,8,256]{2,1,0:T(8,128)S(1)}, f32[4,8,256,256]{2,3,1,0:T(8,128)S(1)}) fusion(f32[4,8,256,256]{2,3,1,0:T(8,128)} %get-tuple-element.297, f32[4,8,256]{2,1,0:T(8,128)} %get-tuple-element.298, bf16[4,256,8,32]{1,3,2,0:T(8,128)(2,1)S(1)} %bitcast.265, bf16[4,256,8,32]{1,3,2,0:T(8,128)(2,1)S(1)} %bitcast.267), kind=kOutput, calls=%fused_computation.2.clone.1 | convolution fusion | flops 140500992 | bytes 17891328 | tf_op jit(solution)/shard_map/while/body/eval_jaxpr/wqhd,wkhd->whqk/dot_general | solution.py:55
  200.3 4.4 multiply_convert_fusion.8
  207.4 2.7 fusion.165
  215.4 29.0 %all_to_all.10 = bf16[32,2,4,2,4,256]{5,4,3,2,1,0:T(4,128)(2,1)S(1)} all-to-all(bf16[32,2,4,2,4,256]{5,4,3,2,1,0:T(4,128)(2,1)S(1)} %bitcast.273), channel_id=1, replica_groups=mesh['row'=8,'col'=4] {'row','col'}, dimensions={0} | all-to-all | bytes 2097152 | tf_op jit(solution)/shard_map/all_to_all | solution.py:213
  250.9 22.4 %fusion.75 = (f32[1024]{0:T(1024)S(1)}, f32[1024]{0:T(1024)S(1)}, f32[1024]{0:T(1024)S(1)}, f32[1024]{0:T(1024)S(1)}, f32[1024]{0:T(1024)S(1)}, /*index=5*/f32[1...) fusion(bf16[34,65,1024]{2,1,0:T(8,128)(2,1)} %copy-done.8, ...), kind=kOutput, calls=%fused_computation.109 | convolution fusion | flops 1151328256 | bytes 52199424 | tf_op jit(solution)/shard_map/dot_general | solution.py:223
  274.3 3.5 collective-permute-start.4
  279.4 6.7 %fusion.83 = f32[1024,256]{1,0:T(8,128)} fusion(f32[32,64,1024]{2,1,0:T(8,128)} %copy-done.9, f32[32,64,256]{2,1,0:T(8,128)} %reshape.182, bf16[32,64,256]{2,1,0:T(8,128)(2,1)S(1)} %copy-done.16), kind=kOutput, calls=%fused_computation.144 | convolution fusion | flops 1085800448 | bytes 12582912 | tf_op jit(solution)/shard_map/dot_general | solution.py:222
  287.7 4.8 %collective-permute-start.7 = (bf16[34,1,1024]{2,1,0:T(2,128)(2,1)S(1)}, bf16[34,1,1024]{2,1,0:T(2,128)(2,1)S(1)}, u32[]{:S(2)}, u32[]{:S(2)}) collective-permute-start(bf16[34,1,1024]{2,1,0:T(2,128)(2,1)S(1)} %get-tuple-element.191), channel_id=1, source_target_pairs={{0,1},{1,2},{2,3},{4,5},{5,6},{6,7},{8,9},{9,10},{10,11},{12,13},{... | collective-permute-start | bytes 208904 | tf_op jit(solution)/shard_map/ppermute | solution.py:20
  295.6 6.1 %pad_maximum_fusion.4 = (bf16[34,65,1024]{2,1,0:T(8,128)(2,1)S(1)}, bf16[34,65,1024]{2,1,0:T(8,128)(2,1)S(1)}) fusion(bf16[34,1,1024]{2,1,0:T(2,128)(2,1)S(1)} %collective-permute-done.6, bf16[1,64,1024]{2,1,0:T(8,128)(2,1)S(1)} %collective-permute-done.5, bf16[32,64,1024]{2,1,0:T(8,128)(2,1)} %bitcast.255, ...), kind=kLoop, calls=%fused_computation.122 | loop fusion | flops 36208640 | bytes 13647872 | tf_op jit(solution)/shard_map/concatenate | solution.py:24
  301.8 12.1 %fusion.67 = f32[32,64,1024]{2,1,0:T(8,128)S(1)} fusion(bf16[32,64,1024]{2,1,0:T(8,128)(2,1)S(1)} %bitcast.257, bf16[34,65,1024]{2,1,0:T(8,128)(2,1)S(1)} %get-tuple-element.189, bf16[1,64,1024]{2,1,0:T(8,128)(2,1)S(1)} %collective-permute-done.4, bf16[34,65,1024]{2,1,0:T(8,128)(2,1)S(1)} %get-tuple-element.188, ...), kind=kLoop, calls=%fused_computation.101 | loop fusion | flops 58720256 | bytes 38047744 | tf_op jit(solution)/shard_map/add | solution.py:85
  313.9 3.5 fusion.62
  319.9 5.5 %multiply_reduce_fusion.4 = (f32[256]{0:T(256)S(1)}, f32[2048]{0:T(1024)S(1)}, f32[2048]{0:T(1024)S(1)}, f32[2048,256]{1,0:T(8,128)}) fusion(bf16[32,64,256]{2,1,0:T(8,128)(2,1)} %param.11, f32[2048]{0:T(1024)S(1)} %copy-done.31, f32[2048]{0:T(1024)S(1)} %copy-done.29, f32[256]{0:T(256)S(1)} %copy-done.52, bf16[2048,1024]{1,0:T(8,128)(2,1)} %copy-done.20, ...), kind=kOutput, calls=%fused_computation.137 | convolution fusion | flops 1078456064 | bytes 7899136 | tf_op jit(solution)/shard_map/dot_general | solution.py:236
  325.4 41.2 %all-reduce = (f32[256]{0:T(256)S(1)}, f32[3,3,1024]{2,1,0:T(4,128)S(1)}, f32[256]{0:T(256)S(1)}) all-reduce(f32[256]{0:T(256)S(1)} %get-tuple-element.146, f32[3,3,1024]{2,1,0:T(4,128)S(1)} %reshape.178, f32[256]{0:T(256)S(1)} %get-tuple-element.64), channel_id=1, replica_groups=mesh['row'=8,'col'=4] {'row','col'}, use_global_device_ids=true, to_apply=%region_15.16 | all-reduce | flops 9728 | bytes 77824 | tf_op jit(solution)/shard_map/psum | solution.py:251
  367.8 3.6 add_convert_fusion.1
  371.4 88.2 %all-reduce.4.cloned.1.call-done = (f32[256,1024]{1,0:T(8,128)}, f32[1024,256]{1,0:T(8,128)}, f32[256,768]{1,0:T(8,128)}, f32[256,256]{1,0:T(8,128)}) async-done(((f32[256,1024]{1,0:T(8,128)}, f32[1024,256]{1,0:T(8,128)}, f32[256,768]{1,0:T(8,128)}, f32[256,256]{1,0:T(8,128)}), (f32[256,1024]{1,0:T(8,128)}, f32[1024,256]{1,0:T(8,128)}, f32[256,768]{1,0:T(8,128)}, ...) | async-done | bytes 3145744 | tf_op jit(solution)/shard_map/psum | solution.py:251
  (233 shorter events, 94.0 us)
Async XLA Ops:
  13.2 17.4 %copy-start.50 = (f32[3,3,1024]{2,1,0:T(4,128)S(1)}, f32[3,3,1024]{2,1,0:T(4,128)}, u32[]{:S(2)}) copy-start(f32[3,3,1024]{2,1,0:T(4,128)} %param.15) | copy-start | bytes 110596
  13.3 17.4 %copy-start.15 = (bf16[32,64,256]{2,1,0:T(8,128)(2,1)S(1)}, bf16[32,64,256]{2,1,0:T(8,128)(2,1)}, u32[]{:S(2)}) copy-start(bf16[32,64,256]{2,1,0:T(8,128)(2,1)} %param.12) | copy-start | bytes 3145732
  17.9 3.7 collective-permute-start
  20.2 5.3 %collective-permute-start.1 = (bf16[1,64,1024]{2,1,0:T(8,128)(2,1)S(1)}, bf16[1,64,1024]{2,1,0:T(8,128)(2,1)S(1)}, u32[]{:S(2)}, u32[]{:S(2)}) collective-permute-start(bf16[1,64,1024]{2,1,0:T(8,128)(2,1)S(1)} %get-tuple-element.199), channel_id=1, source_target_pairs={{4,0},{8,4},{12,8},{16,12},{20,16},{24,20},{28,24},{5,1},{9,5},{13... | collective-permute-start | bytes 393224 | tf_op jit(solution)/shard_map/ppermute | solution.py:23
  21.6 20.4 %copy-start.22 = (bf16[1,64,1024]{2,1,0:T(8,128)(2,1)}, bf16[1,64,1024]{2,1,0:T(8,128)(2,1)S(1)}, u32[]{:S(2)}) copy-start(bf16[1,64,1024]{2,1,0:T(8,128)(2,1)S(1)} %collective-permute-done) | copy-start | bytes 393220
  25.6 16.4 %copy-start.24 = (bf16[1,64,1024]{2,1,0:T(8,128)(2,1)}, bf16[1,64,1024]{2,1,0:T(8,128)(2,1)S(1)}, u32[]{:S(2)}) copy-start(bf16[1,64,1024]{2,1,0:T(8,128)(2,1)S(1)} %collective-permute-done.1) | copy-start | bytes 393220
  25.8 6.1 %collective-permute-start.2 = (bf16[34,1,1024]{2,1,0:T(2,128)(2,1)S(1)}, bf16[34,1,1024]{2,1,0:T(2,128)(2,1)S(1)}, u32[]{:S(2)}, u32[]{:S(2)}) collective-permute-start(bf16[34,1,1024]{2,1,0:T(2,128)(2,1)S(1)} %get-tuple-element.194), channel_id=1, source_target_pairs={{0,1},{1,2},{2,3},{4,5},{5,6},{6,7},{8,9},{9,10},{10,11},{12,13},{... | collective-permute-start | bytes 208904 | tf_op jit(solution)/shard_map/ppermute | solution.py:20
  29.3 6.9 %collective-permute-start.3 = (bf16[34,1,1024]{2,1,0:T(2,128)(2,1)S(1)}, bf16[34,1,1024]{2,1,0:T(2,128)(2,1)S(1)}, u32[]{:S(2)}, u32[]{:S(2)}) collective-permute-start(bf16[34,1,1024]{2,1,0:T(2,128)(2,1)S(1)} %get-tuple-element.195), channel_id=1, source_target_pairs={{1,0},{2,1},{3,2},{5,4},{6,5},{7,6},{9,8},{10,9},{11,10},{13,12},{... | collective-permute-start | bytes 208904 | tf_op jit(solution)/shard_map/ppermute | solution.py:23
  30.7 11.3 %copy-start.32 = (f32[1,1,1024]{2,1,0:T(1,128)}, f32[1,1,1024]{2,1,0:T(1,128)S(1)}, u32[]{:S(2)}) copy-start(f32[1,1,1024]{2,1,0:T(1,128)S(1)} %get-tuple-element.202) | copy-start | bytes 12292
  30.7 11.3 %copy-start.34 = (f32[1,1,1024]{2,1,0:T(1,128)}, f32[1,1,1024]{2,1,0:T(1,128)S(1)}, u32[]{:S(2)}) copy-start(f32[1,1,1024]{2,1,0:T(1,128)S(1)} %get-tuple-element.203) | copy-start | bytes 12292
  30.7 11.3 %copy-start.36 = (f32[1,1,1024]{2,1,0:T(1,128)}, f32[1,1,1024]{2,1,0:T(1,128)S(1)}, u32[]{:S(2)}) copy-start(f32[1,1,1024]{2,1,0:T(1,128)S(1)} %get-tuple-element.204) | copy-start | bytes 12292
  30.7 11.3 %copy-start.38 = (f32[1,1,1024]{2,1,0:T(1,128)}, f32[1,1,1024]{2,1,0:T(1,128)S(1)}, u32[]{:S(2)}) copy-start(f32[1,1,1024]{2,1,0:T(1,128)S(1)} %get-tuple-element.205) | copy-start | bytes 12292
  30.7 11.3 %copy-start.40 = (f32[1,1,1024]{2,1,0:T(1,128)}, f32[1,1,1024]{2,1,0:T(1,128)S(1)}, u32[]{:S(2)}) copy-start(f32[1,1,1024]{2,1,0:T(1,128)S(1)} %get-tuple-element.206) | copy-start | bytes 12292
  30.7 11.3 %copy-start.42 = (f32[1,1,1024]{2,1,0:T(1,128)}, f32[1,1,1024]{2,1,0:T(1,128)S(1)}, u32[]{:S(2)}) copy-start(f32[1,1,1024]{2,1,0:T(1,128)S(1)} %get-tuple-element.207) | copy-start | bytes 12292
  30.7 11.3 %copy-start.44 = (f32[1,1,1024]{2,1,0:T(1,128)}, f32[1,1,1024]{2,1,0:T(1,128)S(1)}, u32[]{:S(2)}) copy-start(f32[1,1,1024]{2,1,0:T(1,128)S(1)} %get-tuple-element.208) | copy-start | bytes 12292
  30.7 11.3 %copy-start.46 = (f32[1,1,1024]{2,1,0:T(1,128)}, f32[1,1,1024]{2,1,0:T(1,128)S(1)}, u32[]{:S(2)}) copy-start(f32[1,1,1024]{2,1,0:T(1,128)S(1)} %get-tuple-element.209) | copy-start | bytes 12292
  41.9 12.2 %copy-start.7 = (bf16[34,65,1024]{2,1,0:T(8,128)(2,1)}, bf16[34,65,1024]{2,1,0:T(8,128)(2,1)S(1)}, u32[]{:S(2)}) copy-start(bf16[34,65,1024]{2,1,0:T(8,128)(2,1)S(1)} %get-tuple-element.192) | copy-start | bytes 13578244
  41.9 12.2 %copy-start.8 = (bf16[34,65,1024]{2,1,0:T(8,128)(2,1)}, bf16[34,65,1024]{2,1,0:T(8,128)(2,1)S(1)}, u32[]{:S(2)}) copy-start(bf16[34,65,1024]{2,1,0:T(8,128)(2,1)S(1)} %get-tuple-element.193) | copy-start | bytes 13578244
  69.0 61.0 %copy-start.21 = (bf16[256,256]{1,0:T(8,128)(2,1)S(1)}, bf16[256,256]{1,0:T(8,128)(2,1)}, u32[]{:S(2)}) copy-start(bf16[256,256]{1,0:T(8,128)(2,1)} %param.19) | copy-start | bytes 393220
  69.0 61.0 %copy-start.51 = (f32[256]{0:T(256)S(1)}, f32[256]{0:T(256)}, u32[]{:S(2)}) copy-start(f32[256]{0:T(256)} %param.17) | copy-start | bytes 3076
  69.0 55.2 %all-to-all-start = ((bf16[2,32,2,4,2,4,256]{6,5,4,3,2,0,1:T(4,128)(2,1)}), bf16[2,32,2,4,2,4,256]{6,5,4,3,2,0,1:T(4,128)(2,1)S(1)}, u32[]{:S(2)}, u32[]{:S(2)}) async-start(bf16[2,32,2,4,2,4,256]{6,5,4,3,2,0,1:T(4,128)(2,1)} %copy.84), calls=%async_computation | async-start | bytes 4194304 | tf_op jit(solution)/shard_map/all_to_all | solution.py:188
  76.7 382.9 %all-reduce.4.cloned.1.call-start = ((), (), s32[]{:S(2)}) async-start(), calls=%async_computation.2 | async-start | bytes 6291456 | tf_op jit(solution)/shard_map/psum | solution.py:251
  213.4 35.3 %copy-start.17 = (f32[256,256]{1,0:T(8,128)}, f32[256,256]{1,0:T(8,128)S(1)}, u32[]{:S(2)}) copy-start(f32[256,256]{1,0:T(8,128)S(1)} %get-tuple-element.66) | copy-start | bytes 786436
  250.9 28.5 %copy-start.16 = (bf16[32,64,256]{2,1,0:T(8,128)(2,1)S(1)}, bf16[32,64,256]{2,1,0:T(8,128)(2,1)}, u32[]{:S(2)}) copy-start(bf16[32,64,256]{2,1,0:T(8,128)(2,1)} %param.12) | copy-start | bytes 3145732
  274.3 11.8 %collective-permute-start.4 = (bf16[1,64,1024]{2,1,0:T(8,128)(2,1)S(1)}, bf16[1,64,1024]{2,1,0:T(8,128)(2,1)S(1)}, u32[]{:S(2)}, u32[]{:S(2)}) collective-permute-start(bf16[1,64,1024]{2,1,0:T(8,128)(2,1)S(1)} %get-tuple-element.196), channel_id=1, source_target_pairs={{0,4},{4,8},{8,12},{12,16},{16,20},{20,24},{24,28},{1,5},{5,9},{9,... | collective-permute-start | bytes 393224 | tf_op jit(solution)/shard_map/ppermute | solution.py:20
  277.8 14.7 %copy-start.4 = (bf16[2048,1024]{1,0:T(8,128)(2,1)S(1)}, bf16[2048,1024]{1,0:T(8,128)(2,1)}, u32[]{:S(2)}) copy-start(bf16[2048,1024]{1,0:T(8,128)(2,1)} %copy-done.2) | copy-start | bytes 12582916
  277.8 8.3 %collective-permute-start.5 = (bf16[1,64,1024]{2,1,0:T(8,128)(2,1)S(1)}, bf16[1,64,1024]{2,1,0:T(8,128)(2,1)S(1)}, u32[]{:S(2)}, u32[]{:S(2)}) collective-permute-start(bf16[1,64,1024]{2,1,0:T(8,128)(2,1)S(1)} %get-tuple-element.197), channel_id=1, source_target_pairs={{4,0},{8,4},{12,8},{16,12},{20,16},{24,20},{28,24},{5,1},{9,5},{13... | collective-permute-start | bytes 393224 | tf_op jit(solution)/shard_map/ppermute | solution.py:23
  286.4 8.4 %collective-permute-start.6 = (bf16[34,1,1024]{2,1,0:T(2,128)(2,1)S(1)}, bf16[34,1,1024]{2,1,0:T(2,128)(2,1)S(1)}, u32[]{:S(2)}, u32[]{:S(2)}) collective-permute-start(bf16[34,1,1024]{2,1,0:T(2,128)(2,1)S(1)} %get-tuple-element.190), channel_id=1, source_target_pairs={{1,0},{2,1},{3,2},{5,4},{6,5},{7,6},{9,8},{10,9},{11,10},{13,12},{... | collective-permute-start | bytes 208904 | tf_op jit(solution)/shard_map/ppermute | solution.py:23
  287.7 7.9 %collective-permute-start.7 = (bf16[34,1,1024]{2,1,0:T(2,128)(2,1)S(1)}, bf16[34,1,1024]{2,1,0:T(2,128)(2,1)S(1)}, u32[]{:S(2)}, u32[]{:S(2)}) collective-permute-start(bf16[34,1,1024]{2,1,0:T(2,128)(2,1)S(1)} %get-tuple-element.191), channel_id=1, source_target_pairs={{0,1},{1,2},{2,3},{4,5},{5,6},{6,7},{8,9},{9,10},{10,11},{12,13},{... | collective-permute-start | bytes 208904 | tf_op jit(solution)/shard_map/ppermute | solution.py:20
  295.6 18.3 %slice-start = ((s8[8388608]{0:T(1024)(128)(4,1)}), s8[4194304]{0:T(1024)(128)(4,1)S(1)}, s32[]{:S(2)}) async-start(s8[8388608]{0:T(1024)(128)(4,1)} %bitcast.258), calls=%async_computation.3 | async-start | bytes 8388608
  301.8 12.1 %slice-start.1 = ((s8[8388608]{0:T(1024)(128)(4,1)}), s8[4194304]{0:T(1024)(128)(4,1)S(1)}, s32[]{:S(2)}) async-start(s8[8388608]{0:T(1024)(128)(4,1)} %bitcast.258), calls=%async_computation.4 | async-start | bytes 8388608
  319.9 47.9 %copy-start.10 = (f32[2048,256]{1,0:T(8,128)S(1)}, f32[2048,256]{1,0:T(8,128)}, u32[]{:S(2)}) copy-start(f32[2048,256]{1,0:T(8,128)} %reshape.181) | copy-start | bytes 6291460
  (40 other events, 225.4 us)
Sparse Core Ops, SparseCore 0:
  320.0 139.6 all-reduce.3
where the time goes:
time: 484 us; the launch traced here: 475 us
  waiting for transfers between devices  146 us (30%)
  matrix products  96.4 us (20%)
  other arithmetic  80.3 us (17%)
  blocking collectives  70.2 us (15%)
  local copies, waits for them, and re-layouts  39.6 us (8%)
  starting transfers between devices  27.5 us (6%)
  between operations  15.4 us (3%)
    psum x1, waiting for transfers between devices, shards(): lax.psum((grad_gain_conv, grad_expand, grad_depth, grad_project, grad_gai...  88.2 us
    all_to_all x1, waiting for transfers between devices, shards(): lax.all_to_all(arranged, ('row', 'col'), split_axis=1, concat_axis=1, til...  47.3 us
    dot_general x20, matrix products, product(): return jnp.einsum(form, left, right, preferred_element_type=jnp.float32)  41.3 us
    psum x1, blocking collectives, shards(): lax.psum((grad_gain_conv, grad_expand, grad_depth, grad_project, grad_gai...  41.2 us
    all_to_all x1, blocking collectives, shards(): lax.all_to_all(arranged, ('row', 'col'), split_axis=0, concat_axis=0, til...  29 us
    dot_general x1, matrix products, shards(): jnp.dot(grad_mid_b, w_project.T, preferred_element_type=jnp.float32)  22.4 us
    ppermute x4, starting transfers between devices, padded_2(): lax.ppermute(lax.slice_in_dim(block, block.shape[dim] - width, None, axis...  14.1 us
    add x1, other arithmetic, spread_back(): summed + grad_pad[2 - row_off:2 - row_off + row_count, 2 - col_off:2 - co...  12.1 us
  transfers between devices with their start and end apart: 10, of which 6 were waited for; matrix products, arithmetic and copies ran while one was open for 4% of the time, Pallas kernels for 0%

commit v1 on v0

v1 whole, which is shorter than its diff:
```python
import jax
import jax.numpy as jnp
from jax import lax
from jax.experimental import pallas as pl
from jax.experimental.pallas import tpu as pltpu
from jax.sharding import PartitionSpec as P

HEADS = 8
GRID = 16


norm_eps = 1e-05
root_half = 0.7071067811865476
inv_root_two_pi = 0.3989422804014327


F32 = jnp.float32
BF16 = jnp.bfloat16
EDGE = 8
BLOCK_E = 256
VMEM_BYTES = 56 * 1024 * 1024


def params():
    return pltpu.CompilerParams(
        dimension_semantics=("arbitrary",), vmem_limit_bytes=VMEM_BYTES
    )


def dot_nn(left, right):
    return lax.dot_general(left, right, (((1,), (0,)), ((), ())), preferred_element_type=F32)


def dot_nt(left, right):
    return lax.dot_general(left, right, (((1,), (1,)), ((), ())), preferred_element_type=F32)


def dot_tn(left, right):
    return lax.dot_general(left, right, (((0,), (0,)), ((), ())), preferred_element_type=F32)


def gelu_parts(values):
    half = 0.5 + 0.5 * lax.erf(values * root_half)
    slope = half + values * jnp.exp(-0.5 * values * values) * inv_root_two_pi
    return values * half, slope


def normalize(values, axis):
    centre = jnp.mean(values, axis=axis, keepdims=True)
    centred = values - centre
    inv_dev = lax.rsqrt(jnp.mean(centred * centred, axis=axis, keepdims=True) + norm_eps)
    return (centred * inv_dev, inv_dev)


def normalize_back(grad_normed, normed, inv_dev, axis):
    return inv_dev * (
        grad_normed
        - jnp.mean(grad_normed, axis=axis, keepdims=True)
        - normed * jnp.mean(grad_normed * normed, axis=axis, keepdims=True)
    )


def full(shape):
    return pl.BlockSpec(shape, lambda step: (0,) * len(shape))


def shift(axis, block, ahead):
    count = lax.axis_size(axis)
    forward = [(i, i + 1) for i in range(count - 1)]
    pairs = forward if ahead else [(target, source) for source, target in forward]
    return lax.ppermute(block, axis, pairs)


def halo(block):
    left = shift("col", block[:, -1:], True)
    right = shift("col", block[:, :1], False)
    wide_last = jnp.concatenate([left[-1:], block[-1:], right[-1:]], axis=1)
    wide_first = jnp.concatenate([left[:1], block[:1], right[:1]], axis=1)
    above = shift("row", wide_last, True)
    below = shift("row", wide_first, False)
    left = jnp.concatenate([above[:, :1], left, below[:, :1]], axis=0)
    right = jnp.concatenate([above[:, -1:], right, below[:, -1:]], axis=0)
    return above[:, 1:-1], below[:, 1:-1], left, right


def conv_forward(ext, core, gain, w_expand, w_taps, w_project, rows, cols):
    chans, expand_w = w_expand.shape
    cells = rows * cols
    around = cols + EDGE
    wide = cols + 2 * EDGE
    steps = expand_w // BLOCK_E

    def kernel(
        ext_ref, core_ref, gain_ref, we_ref, wd_ref, wp_ref,
        hid_out, act_out, sc_out, sp_out, mid_out,
        scaled_ref, pre_ref, hid_ref, acc_ref,
    ):
        step = pl.program_id(0)

        @pl.when(step == 0)
        def _():
            normed, _ = normalize(ext_ref[...].astype(F32), -1)
            scaled_ref[...] = (normed * gain_ref[...]).astype(BF16)
            acc_ref[...] = core_ref[...].astype(F32)

        pre_ref[...] = dot_nn(scaled_ref[...], we_ref[...])

        def put(row, value):
            tail = value[cols:]
            line = jnp.concatenate([tail, value[:cols], tail], axis=0)
            line = line.astype(BF16)
            hid_out[row] = line
            hid_ref[row] = line.astype(F32)

        for row in (0, rows + 1):
            edge = pre_ref[row * around : (row + 1) * around]
            put(row, edge * (0.5 + 0.5 * lax.erf(edge * root_half)))

        def expand_row(index, carry):
            pre = pre_ref[pl.ds(pl.multiple_of((index + 1) * around, 8), around)]
            value, slope = gelu_parts(pre)
            put(index + 1, value)
            sp_out[pl.ds(pl.multiple_of(index * cols, cols), cols)] = slope[:cols].astype(BF16)
            return carry

        lax.fori_loop(0, rows, expand_row, 0)

        def conv_row(index, carry):
            summed = None
            for p in range(3):
                for q in range(3):
                    tap = wd_ref[3 * p + q : 3 * p + q + 1]
                    term = hid_ref[index + p, EDGE - 1 + q : EDGE - 1 + q + cols] * tap
                    summed = term if summed is None else summed + term
            value, slope = gelu_parts(summed)
            here = pl.ds(pl.multiple_of(index * cols, cols), cols)
            act_out[here] = value.astype(BF16)
            sc_out[here] = slope.astype(BF16)
            return carry

        lax.fori_loop(0, rows, conv_row, 0)
        acc_ref[...] += dot_nn(act_out[...], wp_ref[...])

        @pl.when(step == steps - 1)
        def _():
            mid_out[...] = acc_ref[...].astype(BF16)

    ext_cells = (rows + 2) * around
    by_cell = pl.BlockSpec((cells, BLOCK_E), lambda step: (0, step))
    return pl.pallas_call(
        kernel,
        grid=(steps,),
        in_specs=[
            full((ext_cells, chans)),
            full((cells, chans)),
            full((1, chans)),
            pl.BlockSpec((chans, BLOCK_E), lambda step: (0, step)),
            pl.BlockSpec((9, BLOCK_E), lambda step: (0, step)),
            pl.BlockSpec((BLOCK_E, chans), lambda step: (step, 0)),
        ],
        out_specs=[
            pl.BlockSpec((rows + 2, wide, BLOCK_E), lambda step: (0, 0, step)),
            by_cell,
            by_cell,
            by_cell,
            full((cells, chans)),
        ],
        out_shape=[
            jax.ShapeDtypeStruct((rows + 2, wide, expand_w), BF16),
            jax.ShapeDtypeStruct((cells, expand_w), BF16),
            jax.ShapeDtypeStruct((cells, expand_w), BF16),
            jax.ShapeDtypeStruct((cells, expand_w), BF16),
            jax.ShapeDtypeStruct((cells, chans), BF16),
        ],
        scratch_shapes=[
            pltpu.VMEM((ext_cells, chans), BF16),
            pltpu.VMEM((ext_cells, BLOCK_E), F32),
            pltpu.VMEM((rows + 2, wide, BLOCK_E), F32),
            pltpu.VMEM((cells, chans), F32),
        ],
        compiler_params=params(),
        name="conv_forward",
    )(ext, core, gain, w_expand, w_taps, w_project)


def conv_grad(grad_mid_b, w_project, slope):
    cells, chans = grad_mid_b.shape
    expand_w = w_project.shape[0]

    def kernel(gm_ref, wp_ref, slope_ref, out_ref):
        grad_acted = dot_nt(gm_ref[...], wp_ref[...]).astype(BF16).astype(F32)
        out_ref[...] = (grad_acted * slope_ref[...].astype(F32)).astype(BF16)

    by_cell = pl.BlockSpec((cells, BLOCK_E), lambda step: (0, step))
    return pl.pallas_call(
        kernel,
        grid=(expand_w // BLOCK_E,),
        in_specs=[
            full((cells, chans)),
            pl.BlockSpec((BLOCK_E, chans), lambda step: (step, 0)),
            by_cell,
        ],
        out_specs=by_cell,
        out_shape=jax.ShapeDtypeStruct((cells, expand_w), BF16),
        compiler_params=params(),
        name="conv_grad",
    )(grad_mid_b, w_project, slope)


def conv_weight_grads(hidden, acted, grad_conv, grad_mid_t, rows, cols):
    cells, expand_w = acted.shape
    chans = grad_mid_t.shape[0]
    wide = hidden.shape[1]

    def kernel(hid_in, act_ref, gc_ref, gmt_ref, depth_out, proj_out, hid_ref):
        proj_out[...] = dot_nn(gmt_ref[...], act_ref[...])
        hid_ref[...] = hid_in[...].astype(F32)

        def one_row(index, carry):
            grad = gc_ref[pl.ds(pl.multiple_of(index * cols, cols), cols)].astype(F32)
            sums = []
            for p in range(3):
                for q in range(3):
                    term = hid_ref[index + p, EDGE - 1 + q : EDGE - 1 + q + cols] * grad
                    part = term[:8]
                    for low in range(8, cols, 8):
                        part = part + term[low : low + 8]
                    sums.append(carry[3 * p + q] + part)
            return tuple(sums)

        init = tuple(jnp.zeros((8, BLOCK_E), F32) for _ in range(9))
        sums = lax.fori_loop(0, rows, one_row, init)
        for tap in range(9):
            depth_out[tap : tap + 1] = jnp.sum(sums[tap], axis=0, keepdims=True)

    by_cell = pl.BlockSpec((cells, BLOCK_E), lambda step: (0, step))
    return pl.pallas_call(
        kernel,
        grid=(expand_w // BLOCK_E,),
        in_specs=[
            pl.BlockSpec((rows + 2, wide, BLOCK_E), lambda step: (0, 0, step)),
            by_cell,
            by_cell,
            full((chans, cells)),
        ],
        out_specs=[
            pl.BlockSpec((9, BLOCK_E), lambda step: (0, step)),
            pl.BlockSpec((chans, BLOCK_E), lambda step: (0, step)),
        ],
        out_shape=[
            jax.ShapeDtypeStruct((9, expand_w), F32),
            jax.ShapeDtypeStruct((chans, expand_w), F32),
        ],
        scratch_shapes=[pltpu.VMEM((rows + 2, wide, BLOCK_E), F32)],
        compiler_params=params(),
        cost_estimate=pl.CostEstimate(
            flops=2 * cells * expand_w * (chans + 9), bytes_accessed=32 << 20, transcendentals=0
        ),
        name="conv_weight_grads",
    )(hidden, acted, grad_conv, grad_mid_t)


def conv_back(grad_conv, line_pair, side_pair, slope, w_expand, w_taps, core, gain, grad_mid, rows, cols):
    cells, expand_w = grad_conv.shape
    chans = w_expand.shape[0]
    wide = cols + 2 * EDGE
    steps = expand_w // BLOCK_E

    def kernel(
        gc_ref, line_ref, side_ref, slope_ref, we_ref, wd_ref, core_ref, gain_ref, gm_ref,
        expand_out, gain_out, field_out,
        pad_ref, gpre_ref, scaled_t_ref, acc_ref,
    ):
        step = pl.program_id(0)

        @pl.when(step == 0)
        def _():
            normed, _ = normalize(core_ref[...].astype(F32), -1)
            scaled_t_ref[...] = (normed * gain_ref[...]).astype(BF16).T
            acc_ref[...] = jnp.zeros_like(acc_ref)

        def fill(index, carry):
            pad_ref[index + 1, EDGE : EDGE + cols] = gc_ref[
                pl.ds(pl.multiple_of(index * cols, cols), cols)
            ].astype(F32)
            return carry

        lax.fori_loop(0, rows, fill, 0)
        pad_ref[0, EDGE : EDGE + cols] = line_ref[0].astype(F32)
        pad_ref[rows + 1, EDGE : EDGE + cols] = line_ref[1].astype(F32)
        sides = side_ref[...].astype(F32)
        pad_ref[:, :EDGE] = sides[:, :EDGE]
        pad_ref[:, EDGE + cols :] = sides[:, EDGE:]

        def one_row(index, carry):
            summed = None
            for p in range(3):
                for q in range(3):
                    tap = wd_ref[3 * p + q : 3 * p + q + 1]
                    start = EDGE + 1 - q
                    term = pad_ref[index + 2 - p, start : start + cols] * tap
                    summed = term if summed is None else summed + term
            here = pl.ds(pl.multiple_of(index * cols, cols), cols)
            gpre_ref[here] = (summed * slope_ref[here].astype(F32)).astype(BF16)
            return carry

        lax.fori_loop(0, rows, one_row, 0)
        expand_out[...] = dot_nn(scaled_t_ref[...], gpre_ref[...])
        acc_ref[...] += dot_nt(gpre_ref[...], we_ref[...])

        @pl.when(step == steps - 1)
        def _():
            normed, inv_dev = normalize(core_ref[...].astype(F32), -1)
            grad_scaled = acc_ref[...]
            gain_out[...] = jnp.sum(grad_scaled * normed, axis=0, keepdims=True)
            back = normalize_back(grad_scaled * gain_ref[...], normed, inv_dev, -1)
            field_out[...] = (gm_ref[...] + back).astype(BF16)

    by_cell = pl.BlockSpec((cells, BLOCK_E), lambda step: (0, step))
    return pl.pallas_call(
        kernel,
        grid=(steps,),
        in_specs=[
            by_cell,
            pl.BlockSpec((2, cols, BLOCK_E), lambda step: (0, 0, step)),
            pl.BlockSpec((rows + 2, 2 * EDGE, BLOCK_E), lambda step: (0, 0, step)),
            by_cell,
            pl.BlockSpec((chans, BLOCK_E), lambda step: (0, step)),
            pl.BlockSpec((9, BLOCK_E), lambda step: (0, step)),
            full((cells, chans)),
            full((1, chans)),
            full((cells, chans)),
        ],
        out_specs=[
            pl.BlockSpec((chans, BLOCK_E), lambda step: (0, step)),
            full((1, chans)),
            full((cells, chans)),
        ],
        out_shape=[
            jax.ShapeDtypeStruct((chans, expand_w), F32),
            jax.ShapeDtypeStruct((1, chans), F32),
            jax.ShapeDtypeStruct((cells, chans), BF16),
        ],
        scratch_shapes=[
            pltpu.VMEM((rows + 2, wide, BLOCK_E), F32),
            pltpu.VMEM((cells, BLOCK_E), BF16),
            pltpu.VMEM((chans, cells), BF16),
            pltpu.VMEM((cells, chans), F32),
        ],
        compiler_params=params(),
        name="conv_back",
    )(grad_conv, line_pair, side_pair, slope, w_expand, w_taps, core, gain, grad_mid)


def grid_attention(mid_win, cot_win, gain_col, w_qkv, w_qkv_t, w_out):
    sources, windows, each, chans = mid_win.shape
    length = sources * each
    head = chans // HEADS
    scale = head ** (-0.5)

    def kernel(
        mid_ref, cot_ref, gain_ref, wq_ref, wqt_ref, wo_ref,
        branch_out, qkv_out, out_out, gain_out,
        proj_ref, gatt_ref, att_ref, gproj_ref, gg_ref,
    ):
        step = pl.program_id(0)

        @pl.when(step == 0)
        def _():
            qkv_out[...] = jnp.zeros_like(qkv_out)
            out_out[...] = jnp.zeros_like(out_out)
            gg_ref[...] = jnp.zeros_like(gg_ref)

        mid_t = mid_ref[...].astype(F32).reshape(length, chans).T
        cot = cot_ref[...].astype(F32).reshape(length, chans).astype(BF16)
        normed, inv_dev = normalize(mid_t, 0)
        gain = gain_ref[...]
        scaled = (normed * gain).astype(BF16)
        proj_ref[...] = dot_nn(wqt_ref[...], scaled).astype(BF16)
        gatt_ref[...] = dot_nt(wo_ref[...], cot).astype(BF16)
        for h in range(HEADS):
            at_q = slice(h * head, (h + 1) * head)
            at_k = slice(chans + h * head, chans + (h + 1) * head)
            at_v = slice(2 * chans + h * head, 2 * chans + (h + 1) * head)
            query, key, value = proj_ref[at_q], proj_ref[at_k], proj_ref[at_v]
            grad_att = gatt_ref[at_q]
            scores = dot_tn(key, query) * scale
            expons = jnp.exp(scores - jnp.max(scores, axis=0, keepdims=True))
            probs = expons * (1.0 / jnp.sum(expons, axis=0, keepdims=True))
            probs_b = probs.astype(BF16)
            att_ref[at_q] = dot_nn(value, probs_b).astype(BF16)
            gproj_ref[at_v] = dot_nt(grad_att, probs_b).astype(BF16)
            grad_probs = dot_tn(value, grad_att)
            row_sum = jnp.sum(grad_probs * probs, axis=0, keepdims=True)
            grad_scores = (scale * probs * (grad_probs - row_sum)).astype(BF16)
            gproj_ref[at_q] = dot_nn(key, grad_scores).astype(BF16)
            gproj_ref[at_k] = dot_nt(query, grad_scores).astype(BF16)
        out_out[...] += dot_nn(att_ref[...], cot)
        qkv_out[...] += dot_nt(gproj_ref[...], scaled)
        grad_scaled = dot_nn(wq_ref[...], gproj_ref[...])
        gg_ref[...] += grad_scaled * normed
        back = normalize_back(grad_scaled * gain, normed, inv_dev, 0)
        branch_out[...] = back.T.reshape(sources, 1, each, chans).astype(BF16)

        @pl.when(step == windows - 1)
        def _():
            gain_out[...] = jnp.sum(gg_ref[...], axis=1, keepdims=True)

    by_window = pl.BlockSpec((sources, 1, each, chans), lambda step: (0, step, 0, 0))
    return pl.pallas_call(
        kernel,
        grid=(windows,),
        in_specs=[
            by_window,
            by_window,
            full((chans, 1)),
            full((chans, 3 * chans)),
            full((3 * chans, chans)),
            full((chans, chans)),
        ],
        out_specs=[
            by_window,
            full((3 * chans, chans)),
            full((chans, chans)),
            full((chans, 1)),
        ],
        out_shape=[
            jax.ShapeDtypeStruct((sources, windows, each, chans), BF16),
            jax.ShapeDtypeStruct((3 * chans, chans), F32),
            jax.ShapeDtypeStruct((chans, chans), F32),
            jax.ShapeDtypeStruct((chans, 1), F32),
        ],
        scratch_shapes=[
            pltpu.VMEM((3 * chans, length), BF16),
            pltpu.VMEM((chans, length), BF16),
            pltpu.VMEM((chans, length), BF16),
            pltpu.VMEM((3 * chans, length), BF16),
            pltpu.VMEM((chans, length), F32),
        ],
        compiler_params=params(),
        name="grid_attention",
    )(mid_win, cot_win, gain_col, w_qkv, w_qkv_t, w_out)


def shards(field_in, cotangent, gain_conv, w_expand, w_depth, w_project, gain_attn, w_qkv, w_out):
    rows, cols, chans = field_in.shape
    expand_w = w_expand.shape[1]
    cells = rows * cols
    row_devices = lax.axis_size("row")
    col_devices = lax.axis_size("col")
    devices = row_devices * col_devices
    grad_scale = (cells * devices) ** (-0.5)
    per_row = GRID // row_devices
    per_col = GRID // col_devices
    part_rows = rows // per_row // row_devices
    part_cols = cols // per_col // col_devices

    def to_windows(tile):
        arranged = tile.reshape(
            per_row, row_devices, part_rows, per_col, col_devices, part_cols, chans
        )
        arranged = arranged.transpose(1, 4, 2, 5, 0, 3, 6).reshape(
            devices, part_rows * part_cols, per_row * per_col, chans
        )
        return lax.all_to_all(arranged, ("row", "col"), split_axis=0, concat_axis=0, tiled=True)

    cot_win = to_windows(cotangent)
    core = field_in.reshape(cells, chans)
    taps = w_depth.reshape(9, expand_w)
    above, below, left, right = halo(field_in)
    middle = jnp.concatenate([above, field_in, below], axis=0)
    gap = jnp.zeros((rows + 2, EDGE - 2, chans), BF16)
    ext = jnp.concatenate([middle, right, gap, left], axis=1).reshape(-1, chans)
    hidden, acted, slope_conv, slope_pre, mid = conv_forward(
        ext, core, gain_conv.reshape(1, chans), w_expand, taps, w_project, rows, cols
    )
    mid_win = to_windows(mid.reshape(rows, cols, chans))
    branch_win, grad_qkv_t, grad_out, grad_gain_attn = grid_attention(
        mid_win, cot_win, gain_attn.reshape(chans, 1), w_qkv, w_qkv.T, w_out
    )
    moved = lax.all_to_all(branch_win, ("row", "col"), split_axis=0, concat_axis=0, tiled=True)
    moved = moved.reshape(
        row_devices, col_devices, part_rows, part_cols, per_row, per_col, chans
    )
    branch = moved.transpose(4, 0, 2, 5, 1, 3, 6).reshape(cells, chans)
    grad_mid = cotangent.reshape(cells, chans).astype(F32) + branch.astype(F32)
    grad_mid_b = grad_mid.astype(BF16)
    grad_conv = conv_grad(grad_mid_b, w_project, slope_conv)
    above, below, left, right = halo(grad_conv.reshape(rows, cols, expand_w))
    grad_depth, grad_project_t = conv_weight_grads(
        hidden, acted, grad_conv, grad_mid_b.T, rows, cols
    )
    line_pair = jnp.concatenate([above, below], axis=0)
    gap = jnp.zeros((rows + 2, EDGE - 1, expand_w), BF16)
    side_pair = jnp.concatenate([gap, left, right, gap], axis=1)
    grad_expand, grad_gain_conv, grad_field = conv_back(
        grad_conv, line_pair, side_pair, slope_pre, w_expand, taps, core,
        gain_conv.reshape(1, chans), grad_mid, rows, cols,
    )
    sums = sum_over_devices(
        grad_expand, grad_project_t, grad_qkv_t, grad_out, grad_depth,
        grad_gain_conv, grad_gain_attn.reshape(1, chans),
    )
    grad_expand, grad_project_t, grad_qkv_t, grad_out, grad_depth, gain_c, gain_a = [
        value * grad_scale for value in sums
    ]
    return (
        grad_field.reshape(rows, cols, chans),
        gain_c.reshape(chans),
        grad_expand,
        grad_depth.reshape(3, 3, expand_w),
        grad_project_t.T,
        gain_a.reshape(chans),
        grad_qkv_t.T,
        grad_out,
    )


def sum_over_devices(*parts):
    large = [part.astype(BF16) for part in parts[:4]]
    small = parts[4:]
    return [
        value.astype(F32) for value in lax.psum(large, ("row", "col"))
    ] + list(lax.psum(small, ("row", "col")))


def solution(mesh):
    in_specs = (P("row", "col", None), P("row", "col", None), P(), P(), P(), P(), P(), P(), P())
    out_specs = (P("row", "col", None), P(), P(), P(), P(), P(), P(), P())
    return jax.shard_map(shards, mesh=mesh, in_specs=in_specs, out_specs=out_specs, check_vma=False)
```

time: 484 us -> 428 us (0.88); the launches traced: 475 us -> 427 us
  Pallas kernels: 0 us -> 127 us
  matrix products: 96.4 us -> 0 us
  other arithmetic: 80.3 us -> 17.2 us
  blocking collectives: 70.2 us -> 39.3 us
  starting transfers between devices: 27.5 us -> 46.2 us
  local copies, waits for them, and re-layouts: 39.6 us -> 27.8 us
  waiting for transfers between devices: 146 us -> 156 us
    pallas_call x0 -> x5, Pallas kernels: none -> 127 us  [the longest x1 47.2 us: grid_attention(): pl.pallas_call(kernel, grid=(windows,), in_specs=[by_window, by_window, f...]
    dot_general x26 -> x0, matrix products: 85.1 us -> none  [the longest x20 41.3 us: product(): return jnp.einsum(form, left, right, preferred_element_type=jnp.float32)]
    all_to_all x1 -> x0, blocking collectives: 29 us -> none  [shards(): lax.all_to_all(arranged, ('row', 'col'), split_axis=0, concat_axis=0, til...]
    add x5 -> x0, other arithmetic: 26.3 us -> none  [the longest x1 12.1 us: spread_back(): summed + grad_pad[2 - row_off:2 - row_off + row_count, 2 - col_off:2 - co...]
    all_to_all x1 -> x3, starting transfers between devices: 7.69 us -> 26 us  [the longest x2 21.4 us: to_windows(): lax.all_to_all(arranged, ('row', 'col'), split_axis=0, concat_axis=0, til...]
    convert_element_type x7 -> x6, other arithmetic: 24 us -> 8.47 us  [the longest x4 5.69 us: sum_over_devices(): large = [part.astype(BF16) for part in parts[:4]]]
    sub x2 -> x0, matrix products: 11.3 us -> none  [window_back(): scores = scores - jnp.max(scores, axis=-1, keepdims=True)]
    slice x14 -> x16, local copies, waits for them, and re-layouts: 11.9 us -> 2.69 us  [the longest x2 1.54 us: halo(): left = shift('col', block[:, -1:], True)]
  transfers between devices with their start and end apart: 10 -> 12, of which waited for: 6 -> 7; matrix products, arithmetic and copies ran while one was open for 4% -> 4% of each run, Pallas kernels for 0% -> 12%
where the time goes in v1:
time: 428 us; the launch traced here: 427 us
  waiting for transfers between devices  156 us (36%)
  Pallas kernels  127 us (30%)
  starting transfers between devices  46.2 us (11%)
  blocking collectives  39.3 us (9%)
  local copies, waits for them, and re-layouts  27.8 us (6%)
  other arithmetic  17.2 us (4%)
  between operations  14.5 us (3%)
    psum x1, waiting for transfers between devices, sum_over_devices(): lax.psum(large, ('row', 'col'))  90.7 us
    pallas_call x1, Pallas kernels, grid_attention(): pl.pallas_call(kernel, grid=(windows,), in_specs=[by_window, by_window, f...  47.2 us
    psum x1, blocking collectives, sum_over_devices(): lax.psum(small, ('row', 'col'))  39.3 us
    pallas_call x1, Pallas kernels, conv_forward(): pl.pallas_call(kernel, grid=(steps,), in_specs=[full((ext_cells, chans)),...  34.2 us
    pallas_call x1, Pallas kernels, conv_back(): pl.pallas_call(kernel, grid=(steps,), in_specs=[by_cell, pl.BlockSpec((2,...  23.8 us
    all_to_all x2, waiting for transfers between devices, to_windows(): lax.all_to_all(arranged, ('row', 'col'), split_axis=0, concat_axis=0, til...  23.3 us
    all_to_all x1, waiting for transfers between devices, shards(): lax.all_to_all(branch_win, ('row', 'col'), split_axis=0, concat_axis=0, t...  22.7 us
    all_to_all x2, starting transfers between devices, to_windows(): lax.all_to_all(arranged, ('row', 'col'), split_axis=0, concat_axis=0, til...  21.4 us
  transfers between devices with their start and end apart: 12, of which 7 were waited for; matrix products, arithmetic and copies ran while one was open for 4% of the time, Pallas kernels for 12%

profile of v1, /device:TPU:0, one launch (start us, length us, event | category | flops | bytes accessed | tf_op | source)
XLA Modules:
  0.0 427.1 jit_solution(15066010155372917069)
XLA Ops:
  7.2 1.3 reshape.75
  10.2 7.3 %all-to-all-start.1 = ((bf16[32,8,8,256]{3,2,1,0:T(8,128)(2,1)}), bf16[32,8,8,256]{3,2,1,0:T(8,128)(2,1)S(1)}, u32[]{:S(2)}, u32[]{:S(2)}) async-start(bf16[32,8,8,256]{3,2,1,0:T(8,128)(2,1)} %reshape.76), calls=%async_computation.1 | async-start | bytes 2097152 | tf_op jit(solution)/shard_map/all_to_all | solution.py:465
  17.6 3.7 collective-permute-start
  22.6 13.3 %collective-permute-done = bf16[32,1,256]{2,1,0:T(2,128)(2,1)S(1)} collective-permute-done((bf16[32,1,256]{2,1,0:T(2,128)(2,1)S(1)}, bf16[32,1,256]{2,1,0:T(2,128)(2,1)S(1)}, u32[]{:S(2)}, u32[]{:S(2)}) %collective-permute-start) | collective-permute-done | bytes 16416 | tf_op jit(solution)/shard_map/ppermute | solution.py:71
  37.2 3.0 collective-permute-start.2
  41.1 1.4 maximum_maximum_fusion
  42.6 34.2 %conv_forward.1 = (bf16[34,80,1024]{2,1,0:T(8,128)(2,1)}, bf16[2048,1024]{1,0:T(8,128)(2,1)}, bf16[2048,1024]{1,0:T(8,128)(2,1)}, bf16[2048,1024]{1,0:T(8,128)(2,1)}, bf16[2048,256]{1,0:T(8,128)(2,1)}) custom-call(bf16[2448,256]{1,0:T(8,128)(2,1)} %bitcast.38, bf16[2048,256]{1,0:T(8,128)(2,1)} %bitcast.34, f32[1,256]{1,0:T(1,128)} %bitcast.43, ...), custom_call_target="tpu_custom_call" | custom-call | tf_op jit(solution)/shard_map/conv_forward/pallas_call | solution.py:150
  79.8 14.1 %all-to-all-start = ((bf16[32,8,8,256]{3,2,1,0:T(8,128)(2,1)}), bf16[32,8,8,256]{3,2,1,0:T(8,128)(2,1)S(1)}, u32[]{:S(2)}, u32[]{:S(2)}) async-start(bf16[32,8,8,256]{3,2,1,0:T(8,128)(2,1)} %reshape.74), calls=%async_computation | async-start | bytes 2097152 | tf_op jit(solution)/shard_map/all_to_all | solution.py:465
  95.7 23.3 %all-to-all-done.mid_ref = bf16[32,8,8,256]{3,2,1,0:T(8,128)(2,1)S(1)} async-done(((bf16[32,8,8,256]{3,2,1,0:T(8,128)(2,1)}), bf16[32,8,8,256]{3,2,1,0:T(8,128)(2,1)S(1)}, u32[]{:S(2)}, u32[]{:S(2)}) %all-to-all-start) | async-done | bytes 1048608 | tf_op jit(solution)/shard_map/all_to_all | solution.py:465
  120.0 47.2 %grid_attention.1 = (bf16[32,8,8,256]{3,2,1,0:T(8,128)(2,1)}, f32[768,256]{1,0:T(8,128)}, f32[256,256]{1,0:T(8,128)}, f32[256,1]{1,0:T(8,128)}) custom-call(bf16[32,8,8,256]{3,2,1,0:T(8,128)(2,1)} %copy-done.4, bf16[32,8,8,256]{3,2,1,0:T(8,128)(2,1)} %copy-done.3, f32[256,1]{1,0:T(8,128)} %copy.78.gain_ref, bf16[256,768]{1,0:T(8,128)(2,1)} %wq_ref.1, ...), custom_call_target="tpu_custom_call" | custom-call | tf_op jit(solution)/shard_map/grid_attention/pallas_call | solution.py:410
  167.2 4.6 %all-to-all-start.2 = ((bf16[32,8,8,256]{3,2,1,0:T(8,128)(2,1)}), bf16[32,8,8,256]{3,2,1,0:T(8,128)(2,1)}, u32[]{:S(2)}, u32[]{:S(2)}) async-start(bf16[32,8,8,256]{3,2,1,0:T(8,128)(2,1)} %get-tuple-element.23), calls=%async_computation.2 | async-start | bytes 2097152 | tf_op jit(solution)/shard_map/all_to_all | solution.py:481
  172.3 1.8 copy.80
  174.1 22.7 %all-to-all-done.2 = bf16[32,8,8,256]{3,2,1,0:T(8,128)(2,1)} async-done(((bf16[32,8,8,256]{3,2,1,0:T(8,128)(2,1)}), bf16[32,8,8,256]{3,2,1,0:T(8,128)(2,1)}, u32[]{:S(2)}, u32[]{:S(2)}) %all-to-all-start.2) | async-done | bytes 1048608 | tf_op jit(solution)/shard_map/all_to_all | solution.py:481
  196.8 1.6 reshape.86
  198.4 2.1 copy.89
  200.5 2.0 reshape.85
  202.5 1.8 copy.81
  204.4 2.6 fusion
  208.3 6.2 %conv_grad.1.gc_ref = bf16[2048,1024]{1,0:T(8,128)(2,1)} custom-call(bf16[2048,256]{1,0:T(8,128)(2,1)} %copy.82.gm_ref, bf16[1024,256]{1,0:T(8,128)(2,1)} %wp_ref.3, bf16[2048,1024]{1,0:T(8,128)(2,1)} %get-tuple-element.24.slope_ref), custom_call_target="tpu_custom_call" | custom-call | tf_op jit(solution)/shard_map/conv_grad/pallas_call | solution.py:195
  214.5 1.5 fusion.1
  216.0 5.0 %collective-permute-start.4 = (bf16[32,1,1024]{2,1,0:T(2,128)(2,1)S(1)}, bf16[32,1,1024]{2,1,0:T(2,128)(2,1)S(1)}, u32[]{:S(2)}, u32[]{:S(2)}) collective-permute-start(bf16[32,1,1024]{2,1,0:T(2,128)(2,1)S(1)} %get-tuple-element.87), channel_id=1, source_target_pairs={{0,1},{1,2},{2,3},{4,5},{5,6},{6,7},{8,9},{9,10},{10,11},{12,13},{... | collective-permute-start | bytes 196616 | tf_op jit(solution)/shard_map/ppermute | solution.py:71
  223.5 5.3 %collective-permute-done.5 = bf16[32,1,1024]{2,1,0:T(2,128)(2,1)S(1)} collective-permute-done((bf16[32,1,1024]{2,1,0:T(2,128)(2,1)S(1)}, bf16[32,1,1024]{2,1,0:T(2,128)(2,1)S(1)}, u32[]{:S(2)}, u32[]{:S(2)}) %collective-permute-start.5) | collective-permute-done | bytes 65568 | tf_op jit(solution)/shard_map/ppermute | solution.py:71
  230.3 3.0 collective-permute-start.6
  234.8 1.8 copy.83.gm_ref
  236.6 15.0 %conv_weight_grads.1 = (f32[9,1024]{1,0:T(8,128)}, f32[256,1024]{1,0:T(8,128)}) custom-call(bf16[34,80,1024]{2,1,0:T(8,128)(2,1)} %get-tuple-element.29.hid_in, bf16[2048,1024]{1,0:T(8,128)(2,1)} %get-tuple-element.30.act_ref, bf16[2048,1024]{1,0:T(8,128)(2,1)} %conv_grad.1.gc_ref, bf16[256,2048]{1,0:T(8,128)(2,1)} %bitcast.36), custom_call_target="tpu_custom_call" | custom-call | flops 1111490560 | bytes 33554432 | tf_op jit(solution)/shard_map/conv_weight_grads/pallas_call | solution.py:237
  251.7 2.1 convert_element_type.54
  254.7 1.7 pad_maximum_fusion.side_ref
  256.4 23.8 %conv_back.1 = (f32[256,1024]{1,0:T(8,128)}, f32[1,256]{1,0:T(1,128)}, bf16[2048,256]{1,0:T(8,128)(2,1)}) custom-call(bf16[2048,1024]{1,0:T(8,128)(2,1)} %conv_grad.1.gc_ref, bf16[2,64,1024]{2,1,0:T(8,128)(2,1)} %pad_maximum_fusion.1.line_ref, bf16[34,16,1024]{2,1,0:T(8,128)(2,1)} %pad_maximum_fusion.side_ref, ...), custom_call_target="tpu_custom_call" | custom-call | tf_op jit(solution)/shard_map/conv_back/pallas_call | solution.py:320
  280.3 2.1 convert_element_type.52
  282.6 39.3 %all-reduce = (f32[1,256]{1,0:T(1,128)S(1)}, f32[9,1024]{1,0:T(8,128)S(1)}, f32[1,256]{1,0:T(1,128)S(1)}) all-reduce(f32[1,256]{1,0:T(1,128)S(1)} %copy-done.14, f32[9,1024]{1,0:T(8,128)S(1)} %copy-done.11, f32[1,256]{1,0:T(1,128)S(1)} %bitcast.42), channel_id=1, replica_groups=mesh['row'=8,'col'=4] {'row','col'}, use_global_device_ids=true, to_apply=%region_0.0 | all-reduce | flops 9728 | bytes 77824 | tf_op jit(solution)/shard_map/psum | solution.py:524
  323.1 90.7 %all-reduce.4.cloned.1.call-done = (bf16[256,1024]{1,0:T(8,128)(2,1)}, bf16[256,1024]{1,0:T(8,128)(2,1)}, bf16[768,256]{1,0:T(8,128)(2,1)}, bf16[256,256]{1,0:T(8,128)(2,1)}) async-done(((bf16[256,1024]{1,0:T(8,128)(2,1)}, bf16[256,1024]{1,0:T(8,128)(2,1)}, bf16[768,256]{1,0:T(8,128)(2,1)}, bf16[256,256]{1,0:T(8,128)(2,1)}), (bf16[256,1024]{1,0:T(8,128)(2,1)}, bf16[256,1024]{1,0:T(8,128)(2,1)}, ...) | async-done | bytes 1572880 | tf_op jit(solution)/shard_map/psum | solution.py:523
  413.8 1.7 convert_multiply_fusion.1
  (86 shorter events, 25.0 us)
Async XLA Ops:
  9.1 8.4 %copy-start = (bf16[32,64,256]{2,1,0:T(8,128)(2,1)S(1)}, bf16[32,64,256]{2,1,0:T(8,128)(2,1)}, u32[]{:S(2)}) copy-start(bf16[32,64,256]{2,1,0:T(8,128)(2,1)} %param.9) | copy-start | bytes 3145732
  9.1 31.2 %copy-start.12 = (f32[3,3,1024]{2,1,0:T(4,128)S(1)}, f32[3,3,1024]{2,1,0:T(4,128)}, u32[]{:S(2)}) copy-start(f32[3,3,1024]{2,1,0:T(4,128)} %param.13) | copy-start | bytes 110596
  10.2 69.6 %all-to-all-start.1 = ((bf16[32,8,8,256]{3,2,1,0:T(8,128)(2,1)}), bf16[32,8,8,256]{3,2,1,0:T(8,128)(2,1)S(1)}, u32[]{:S(2)}, u32[]{:S(2)}) async-start(bf16[32,8,8,256]{3,2,1,0:T(8,128)(2,1)} %reshape.76), calls=%async_computation.1 | async-start | bytes 2097152 | tf_op jit(solution)/shard_map/all_to_all | solution.py:465
  17.6 18.3 %collective-permute-start = (bf16[32,1,256]{2,1,0:T(2,128)(2,1)S(1)}, bf16[32,1,256]{2,1,0:T(2,128)(2,1)S(1)}, u32[]{:S(2)}, u32[]{:S(2)}) collective-permute-start(bf16[32,1,256]{2,1,0:T(2,128)(2,1)S(1)} %get-tuple-element.91), channel_id=1, source_target_pairs={{0,1},{1,2},{2,3},{4,5},{5,6},{6,7},{8,9},{9,10},{10,11},{12,13},{... | collective-permute-start | bytes 49160 | tf_op jit(solution)/shard_map/ppermute | solution.py:71
  21.3 14.6 %collective-permute-start.1 = (bf16[32,1,256]{2,1,0:T(2,128)(2,1)S(1)}, bf16[32,1,256]{2,1,0:T(2,128)(2,1)S(1)}, u32[]{:S(2)}, u32[]{:S(2)}) collective-permute-start(bf16[32,1,256]{2,1,0:T(2,128)(2,1)S(1)} %get-tuple-element.92), channel_id=1, source_target_pairs={{1,0},{2,1},{3,2},{5,4},{6,5},{7,6},{9,8},{10,9},{11,10},{13,12},{... | collective-permute-start | bytes 49160 | tf_op jit(solution)/shard_map/ppermute | solution.py:71
  35.9 5.1 %collective-permute-start.3 = (bf16[1,66,256]{2,1,0:T(8,128)(2,1)S(1)}, bf16[1,66,256]{2,1,0:T(8,128)(2,1)S(1)}, u32[]{:S(2)}, u32[]{:S(2)}) collective-permute-start(bf16[1,66,256]{2,1,0:T(8,128)(2,1)S(1)} %pad_maximum_fusion.5), channel_id=1, source_target_pairs={{4,0},{8,4},{12,8},{16,12},{20,16},{24,20},{28,24},{5,1},{9,5},{13... | collective-permute-start | bytes 101384 | tf_op jit(solution)/shard_map/ppermute | solution.py:71
  37.2 3.9 collective-permute-start.2
  78.7 15.3 %copy-start.13 = (f32[256]{0:T(256)S(1)}, f32[256]{0:T(256)}, u32[]{:S(2)}) copy-start(f32[256]{0:T(256)} %param.15) | copy-start | bytes 3076
  78.7 16.1 %copy-start.5 = (bf16[256,768]{1,0:T(8,128)(2,1)S(1)}, bf16[256,768]{1,0:T(8,128)(2,1)}, u32[]{:S(2)}) copy-start(bf16[256,768]{1,0:T(8,128)(2,1)} %wq_ref.1) | copy-start | bytes 1179652
  79.8 39.2 %copy-start.3 = (bf16[32,8,8,256]{3,2,1,0:T(8,128)(2,1)}, bf16[32,8,8,256]{3,2,1,0:T(8,128)(2,1)S(1)}, u32[]{:S(2)}) copy-start(bf16[32,8,8,256]{3,2,1,0:T(8,128)(2,1)S(1)} %all-to-all-done.1.cot_ref) | copy-start | bytes 3145732
  79.8 39.2 %all-to-all-start = ((bf16[32,8,8,256]{3,2,1,0:T(8,128)(2,1)}), bf16[32,8,8,256]{3,2,1,0:T(8,128)(2,1)S(1)}, u32[]{:S(2)}, u32[]{:S(2)}) async-start(bf16[32,8,8,256]{3,2,1,0:T(8,128)(2,1)} %reshape.74), calls=%async_computation | async-start | bytes 2097152 | tf_op jit(solution)/shard_map/all_to_all | solution.py:465
  119.0 1.0 copy-start.4
  120.0 52.0 %copy-start.2 = (bf16[32,64,256]{2,1,0:T(8,128)(2,1)S(1)}, bf16[32,64,256]{2,1,0:T(8,128)(2,1)}, u32[]{:S(2)}) copy-start(bf16[32,64,256]{2,1,0:T(8,128)(2,1)} %param.10) | copy-start | bytes 3145732
  167.2 29.6 %all-to-all-start.2 = ((bf16[32,8,8,256]{3,2,1,0:T(8,128)(2,1)}), bf16[32,8,8,256]{3,2,1,0:T(8,128)(2,1)}, u32[]{:S(2)}, u32[]{:S(2)}) async-start(bf16[32,8,8,256]{3,2,1,0:T(8,128)(2,1)} %get-tuple-element.23), calls=%async_computation.2 | async-start | bytes 2097152 | tf_op jit(solution)/shard_map/all_to_all | solution.py:481
  171.8 242.0 %all-reduce.4.cloned.1.call-start = ((), (), s32[]{:S(2)}) async-start(), calls=%async_computation.3 | async-start | bytes 3145728 | tf_op jit(solution)/shard_map/psum | solution.py:523
  206.9 7.6 %copy-start.1 = (bf16[2048,256]{0,1:T(8,128)(2,1)}, bf16[2048,256]{0,1:T(8,128)(2,1)S(1)}, u32[]{:S(2)}) copy-start(bf16[2048,256]{0,1:T(8,128)(2,1)S(1)} %get-tuple-element.83) | copy-start | bytes 3145732
  208.3 25.1 %copy-start.9 = (f32[256,256]{1,0:T(8,128)S(1)}, f32[256,256]{1,0:T(8,128)}, u32[]{:S(2)}) copy-start(f32[256,256]{1,0:T(8,128)} %get-tuple-element.35) | copy-start | bytes 786436
  214.5 19.5 %copy-start.6 = (f32[768,256]{1,0:T(8,128)S(1)}, f32[768,256]{1,0:T(8,128)}, u32[]{:S(2)}) copy-start(f32[768,256]{1,0:T(8,128)} %get-tuple-element.34) | copy-start | bytes 2359300
  216.0 7.5 %collective-permute-start.4 = (bf16[32,1,1024]{2,1,0:T(2,128)(2,1)S(1)}, bf16[32,1,1024]{2,1,0:T(2,128)(2,1)S(1)}, u32[]{:S(2)}, u32[]{:S(2)}) collective-permute-start(bf16[32,1,1024]{2,1,0:T(2,128)(2,1)S(1)} %get-tuple-element.87), channel_id=1, source_target_pairs={{0,1},{1,2},{2,3},{4,5},{5,6},{6,7},{8,9},{9,10},{10,11},{12,13},{... | collective-permute-start | bytes 196616 | tf_op jit(solution)/shard_map/ppermute | solution.py:71
  222.0 6.9 %collective-permute-start.5 = (bf16[32,1,1024]{2,1,0:T(2,128)(2,1)S(1)}, bf16[32,1,1024]{2,1,0:T(2,128)(2,1)S(1)}, u32[]{:S(2)}, u32[]{:S(2)}) collective-permute-start(bf16[32,1,1024]{2,1,0:T(2,128)(2,1)S(1)} %get-tuple-element.88), channel_id=1, source_target_pairs={{1,0},{2,1},{3,2},{5,4},{6,5},{7,6},{9,8},{10,9},{11,10},{13,12},{... | collective-permute-start | bytes 196616 | tf_op jit(solution)/shard_map/ppermute | solution.py:71
  228.9 24.8 %collective-permute-start.7 = (bf16[1,66,1024]{2,1,0:T(8,128)(2,1)S(1)}, bf16[1,66,1024]{2,1,0:T(8,128)(2,1)S(1)}, u32[]{:S(2)}, u32[]{:S(2)}) collective-permute-start(bf16[1,66,1024]{2,1,0:T(8,128)(2,1)S(1)} %pad_maximum_fusion.3), channel_id=1, source_target_pairs={{4,0},{8,4},{12,8},{16,12},{20,16},{24,20},{28,24},{5,1},{9,5},{13... | collective-permute-start | bytes 405512 | tf_op jit(solution)/shard_map/ppermute | solution.py:71
  230.3 23.5 %collective-permute-start.6 = (bf16[1,66,1024]{2,1,0:T(8,128)(2,1)S(1)}, bf16[1,66,1024]{2,1,0:T(8,128)(2,1)S(1)}, u32[]{:S(2)}, u32[]{:S(2)}) collective-permute-start(bf16[1,66,1024]{2,1,0:T(8,128)(2,1)S(1)} %pad_maximum_fusion.2), channel_id=1, source_target_pairs={{0,4},{4,8},{8,12},{12,16},{16,20},{20,24},{24,28},{1,5},{5,9},{9,... | collective-permute-start | bytes 405512 | tf_op jit(solution)/shard_map/ppermute | solution.py:71
  280.2 2.2 copy-start.10
  280.2 2.3 copy-start.11
  280.2 2.3 copy-start.14
  413.8 3.9 copy-start.7
  413.8 3.9 copy-start.8
Sparse Core Ops, SparseCore 0:
  282.5 131.1 all-reduce.3

commit v2 on v1

--- a/solution.py
+++ b/solution.py
@@ -245,11 +245,11 @@
         ],
         out_specs=[
             pl.BlockSpec((9, BLOCK_E), lambda step: (0, step)),
-            pl.BlockSpec((chans, BLOCK_E), lambda step: (0, step)),
+            pl.BlockSpec((chans, BLOCK_E), lambda step: (step, 0)),
         ],
         out_shape=[
             jax.ShapeDtypeStruct((9, expand_w), F32),
-            jax.ShapeDtypeStruct((chans, expand_w), F32),
+            jax.ShapeDtypeStruct((expand_w // BLOCK_E * chans, BLOCK_E), F32),
         ],
         scratch_shapes=[pltpu.VMEM((rows + 2, wide, BLOCK_E), F32)],
         compiler_params=params(),
@@ -332,12 +332,12 @@
             full((cells, chans)),
         ],
         out_specs=[
-            pl.BlockSpec((chans, BLOCK_E), lambda step: (0, step)),
+            pl.BlockSpec((chans, BLOCK_E), lambda step: (step, 0)),
             full((1, chans)),
             full((cells, chans)),
         ],
         out_shape=[
-            jax.ShapeDtypeStruct((chans, expand_w), F32),
+            jax.ShapeDtypeStruct((steps * chans, BLOCK_E), F32),
             jax.ShapeDtypeStruct((1, chans), F32),
             jax.ShapeDtypeStruct((cells, chans), BF16),
         ],
@@ -464,13 +464,14 @@
         )
         return lax.all_to_all(arranged, ("row", "col"), split_axis=0, concat_axis=0, tiled=True)
 
-    cot_win = to_windows(cotangent)
     core = field_in.reshape(cells, chans)
     taps = w_depth.reshape(9, expand_w)
     above, below, left, right = halo(field_in)
     middle = jnp.concatenate([above, field_in, below], axis=0)
     gap = jnp.zeros((rows + 2, EDGE - 2, chans), BF16)
     ext = jnp.concatenate([middle, right, gap, left], axis=1).reshape(-1, chans)
+    held, ext = lax.optimization_barrier((cotangent, ext))
+    cot_win = to_windows(held)
     hidden, acted, slope_conv, slope_pre, mid = conv_forward(
         ext, core, gain_conv.reshape(1, chans), w_expand, taps, w_project, rows, cols
     )
@@ -497,31 +498,173 @@
         grad_conv, line_pair, side_pair, slope_pre, w_expand, taps, core,
         gain_conv.reshape(1, chans), grad_mid, rows, cols,
     )
-    sums = sum_over_devices(
-        grad_expand, grad_project_t, grad_qkv_t, grad_out, grad_depth,
-        grad_gain_conv, grad_gain_attn.reshape(1, chans),
-    )
-    grad_expand, grad_project_t, grad_qkv_t, grad_out, grad_depth, gain_c, gain_a = [
-        value * grad_scale for value in sums
-    ]
+    small_rows = 9 * expand_w // chans
+    small = jnp.concatenate(
+        [
+            grad_depth.reshape(small_rows, chans),
+            grad_gain_conv,
+            grad_gain_attn.reshape(1, chans),
+            jnp.zeros((-(small_rows + 2) % 8, chans), F32),
+        ]
+    )
+    grad_expand, grad_project, grad_qkv, grad_out, small = sum_over_devices(
+        grad_expand, grad_project_t, grad_qkv_t, grad_out, small, grad_scale
+    )
     return (
         grad_field.reshape(rows, cols, chans),
-        gain_c.reshape(chans),
+        small[small_rows],
         grad_expand,
-        grad_depth.reshape(3, 3, expand_w),
-        grad_project_t.T,
-        gain_a.reshape(chans),
-        grad_qkv_t.T,
+        small[:small_rows].reshape(3, 3, expand_w),
+        grad_project,
+        small[small_rows + 1],
+        grad_qkv,
         grad_out,
     )
 
 
-def sum_over_devices(*parts):
-    large = [part.astype(BF16) for part in parts[:4]]
-    small = parts[4:]
-    return [
-        value.astype(F32) for value in lax.psum(large, ("row", "col"))
-    ] + list(lax.psum(small, ("row", "col")))
+def sum_over_devices(expand, project_t, qkv_t, out, small, grad_scale):
+    lanes = 128
+    chans = out.shape[0]
+    halves = out.shape[1] // lanes
+    parts = (expand, project_t, qkv_t, out, small)
+    starts = [0]
+    for part in parts:
+        starts.append(starts[-1] + part.shape[0])
+    blocks = expand.shape[0] // chans
+    sizes = {axis: lax.axis_size(axis) for axis in ("row", "col")}
+    devices = sizes["row"] * sizes["col"]
+    unit = 16 * devices
+    total = -(-starts[-1] // unit) * unit
+    row_bits = [("row", bit) for bit in range(sizes["row"].bit_length() - 1)]
+    col_bits = [("col", bit) for bit in range(sizes["col"].bit_length() - 1)]
+    orders = [row_bits + col_bits, row_bits[:1] + col_bits + row_bits[1:]]
+    count = len(orders[0])
+
+    def kernel(
+        ex_ref, pr_ref, qk_ref, ou_ref, sm_ref,
+        ex_out, pr_out, qk_out, ou_out, sm_out,
+        acc_ref, send_ref, recv_ref, got_ref, send_sem, recv_sem,
+    ):
+        places = {"row": lax.axis_index("row"), "col": lax.axis_index("col")}
+
+        def partner(axis, bit):
+            mine = lax.rem(places[axis] // (1 << bit), 2)
+            return mine, {axis: places[axis] + (1 - 2 * mine) * (1 << bit)}
+
+        barrier = pltpu.get_barrier_semaphore()
+        for axis, bit in orders[0]:
+            _, target = partner(axis, bit)
+            pl.semaphore_signal(
+                barrier, inc=1, device_id=target, device_id_type=pl.DeviceIdType.MESH
+            )
+        pl.semaphore_wait(barrier, count)
+
+        for lane in range(halves):
+            span = slice(lane * lanes, (lane + 1) * lanes)
+            for start, ref in zip(starts, (ex_ref, pr_ref, qk_ref, ou_ref, sm_ref)):
+                acc_ref[lane, start : start + ref.shape[0]] = ref[:, span]
+            if total > starts[-1]:
+                acc_ref[lane, starts[-1] : total] = jnp.zeros((total - starts[-1], lanes), F32)
+
+        offsets = [0] * halves
+
+        def reduce_start(lane, step):
+            size = total >> (step + 1)
+            mine, target = partner(*orders[lane % 2][step])
+            away = pl.multiple_of(offsets[lane] + (1 - mine) * size, 16)
+            offsets[lane] = pl.multiple_of(offsets[lane] + mine * size, 16)
+            send_ref[lane, pl.ds(away, size)] = acc_ref[lane, pl.ds(away, size)].astype(BF16)
+            copy = pltpu.make_async_remote_copy(
+                src_ref=send_ref.at[lane, pl.ds(away, size)],
+                dst_ref=recv_ref.at[lane, pl.ds(total - 2 * size, size)],
+                send_sem=send_sem.at[lane, step],
+                recv_sem=recv_sem.at[lane, step],
+                device_id=target,
+                device_id_type=pl.DeviceIdType.MESH,
+            )
+            copy.start()
+            return copy
+
+        def reduce_end(lane, step, copy):
+            size = total >> (step + 1)
+            copy.wait()
+            kept = pl.ds(offsets[lane], size)
+            acc_ref[lane, kept] += recv_ref[lane, pl.ds(total - 2 * size, size)].astype(F32)
+
+        copies = [reduce_start(lane, 0) for lane in range(halves)]
+        for step in range(count):
+            for lane in range(halves):
+                reduce_end(lane, step, copies[lane])
+                if step + 1 < count:
+                    copies[lane] = reduce_start(lane, step + 1)
+
+        def gather_start(lane, step):
+            size = total >> (step + 1)
+            mine, target = partner(*orders[lane % 2][step])
+            own = pl.ds(offsets[lane], size)
+            copy = pltpu.make_async_remote_copy(
+                src_ref=got_ref.at[lane, own],
+                dst_ref=got_ref.at[lane, own],
+                send_sem=send_sem.at[lane, count + step],
+                recv_sem=recv_sem.at[lane, count + step],
+                device_id=target,
+                device_id_type=pl.DeviceIdType.MESH,
+            )
+            copy.start()
+            offsets[lane] = pl.multiple_of(offsets[lane] - mine * size, 16)
+            return copy
+
+        for lane in range(halves):
+            own = pl.ds(offsets[lane], total >> count)
+            got_ref[lane, own] = (acc_ref[lane, own] * grad_scale).astype(BF16)
+            copies[lane] = gather_start(lane, count - 1)
+        for step in reversed(range(count)):
+            for lane in range(halves):
+                copies[lane].wait()
+                if step:
+                    copies[lane] = gather_start(lane, step - 1)
+
+        def read(start, size):
+            return jnp.concatenate(
+                [got_ref[lane, start : start + size].astype(F32) for lane in range(halves)], axis=1
+            )
+
+        for block in range(blocks):
+            low, high = block * chans, (block + 1) * chans
+            ex_out[:, low:high] = read(starts[0] + low, chans)
+            pr_out[low:high] = read(starts[1] + low, chans).T
+        for block in range(qkv_t.shape[0] // chans):
+            low, high = block * chans, (block + 1) * chans
+            qk_out[:, low:high] = read(starts[2] + low, chans).T
+        ou_out[...] = read(starts[3], chans)
+        packed = -(-small.shape[0] // 16) * 16
+        sm_out[...] = read(starts[4], packed)[: small.shape[0]]
+
+    whole = [pl.BlockSpec(memory_space=pltpu.VMEM)] * 5
+    return pl.pallas_call(
+        kernel,
+        in_specs=whole,
+        out_specs=whole,
+        out_shape=[
+            jax.ShapeDtypeStruct((chans, blocks * chans), F32),
+            jax.ShapeDtypeStruct((blocks * chans, chans), F32),
+            jax.ShapeDtypeStruct((chans, qkv_t.shape[0]), F32),
+            jax.ShapeDtypeStruct(out.shape, F32),
+            jax.ShapeDtypeStruct(small.shape, F32),
+        ],
+        scratch_shapes=[
+            pltpu.VMEM((halves, total, lanes), F32),
+            pltpu.VMEM((halves, total, lanes), BF16),
+            pltpu.VMEM((halves, total, lanes), BF16),
+            pltpu.VMEM((halves, total, lanes), BF16),
+            pltpu.SemaphoreType.DMA((halves, 2 * count)),
+            pltpu.SemaphoreType.DMA((halves, 2 * count)),
+        ],
+        compiler_params=pltpu.CompilerParams(
+            collective_id=0, has_side_effects=True, vmem_limit_bytes=VMEM_BYTES
+        ),
+        name="sum_over_devices",
+    )(*parts)
 
 
 def solution(mesh):

time: 428 us -> 336 us (0.79)
  waiting for transfers between devices: 156 us -> 78.4 us
  Pallas kernels: 127 us -> 176 us
  blocking collectives: 39.3 us -> 0 us
  between operations: 14.5 us -> 0.99 us
  starting transfers between devices: 46.2 us -> 34 us
  local copies, waits for them, and re-layouts: 27.8 us -> 36.9 us
  other arithmetic: 17.2 us -> 9.33 us
    psum x1 -> x0, waiting for transfers between devices: 90.7 us -> none  [sum_over_devices(): lax.psum(large, ('row', 'col'))]
    pallas_call x0 -> x1, Pallas kernels: none -> 49.3 us  [sum_over_devices(): pl.pallas_call(kernel, in_specs=whole, out_specs=whole, out_shape=[jax.Sh...]
    psum x1 -> x0, blocking collectives: 39.3 us -> none  [sum_over_devices(): lax.psum(small, ('row', 'col'))]
    all_to_all x2, waiting for transfers between devices: 23.3 us -> 44.3 us  [to_windows(): lax.all_to_all(arranged, ('row', 'col'), split_axis=0, concat_axis=0, til...]
    all_to_all x2, starting transfers between devices: 21.4 us -> 11.5 us  [to_windows(): lax.all_to_all(arranged, ('row', 'col'), split_axis=0, concat_axis=0, til...]
    ppermute x8, waiting for transfers between devices: 18.9 us -> 11.2 us  [shift(): return lax.ppermute(block, axis, pairs)]
    convert_element_type x4 -> x0, other arithmetic: 5.69 us -> none  [sum_over_devices(): large = [part.astype(BF16) for part in parts[:4]]]
  transfers between devices with their start and end apart: 12 -> 11, of which waited for: 7 -> 7; matrix products, arithmetic and copies ran while one was open for 4% -> 4% of each run, Pallas kernels for 12% -> 4%
where the time goes in v2:
time: 336 us; the launch traced here: 335 us
  Pallas kernels  176 us (52%)
  waiting for transfers between devices  78.4 us (23%)
  local copies, waits for them, and re-layouts  36.9 us (11%)
  starting transfers between devices  34 us (10%)
  other arithmetic  9.33 us (3%)
    pallas_call x1, Pallas kernels, sum_over_devices(): pl.pallas_call(kernel, in_specs=whole, out_specs=whole, out_shape=[jax.Sh...  49.3 us
    pallas_call x1, Pallas kernels, grid_attention(): pl.pallas_call(kernel, grid=(windows,), in_specs=[by_window, by_window, f...  47.1 us
    all_to_all x2, waiting for transfers between devices, to_windows(): lax.all_to_all(arranged, ('row', 'col'), split_axis=0, concat_axis=0, til...  44.3 us
    pallas_call x1, Pallas kernels, conv_forward(): pl.pallas_call(kernel, grid=(steps,), in_specs=[full((ext_cells, chans)),...  34.2 us
    pallas_call x1, Pallas kernels, conv_back(): pl.pallas_call(kernel, grid=(steps,), in_specs=[by_cell, pl.BlockSpec((2,...  23.8 us
    all_to_all x1, waiting for transfers between devices, shards(): lax.all_to_all(branch_win, ('row', 'col'), split_axis=0, concat_axis=0, t...  22.8 us
    ppermute x8, starting transfers between devices, shift(): return lax.ppermute(block, axis, pairs)  17.7 us
    pallas_call x1, Pallas kernels, conv_weight_grads(): pl.pallas_call(kernel, grid=(expand_w // BLOCK_E,), in_specs=[pl.BlockSpe...  15.1 us
  transfers between devices with their start and end apart: 11, of which 7 were waited for; matrix products, arithmetic and copies ran while one was open for 4% of the time, Pallas kernels for 4%

profile of v2, /device:TPU:0, one launch (start us, length us, event | category | flops | bytes accessed | tf_op | source)
XLA Modules:
  0.0 335.3 jit_solution(7727795376266289752)
XLA Ops:
  1.7 4.9 %collective-permute-start = (bf16[32,1,256]{2,1,0:T(2,128)(2,1)S(1)}, bf16[32,1,256]{2,1,0:T(2,128)(2,1)S(1)}, u32[]{:S(2)}, u32[]{:S(2)}) collective-permute-start(bf16[32,1,256]{2,1,0:T(2,128)(2,1)S(1)} %get-tuple-element.58), channel_id=1, source_target_pairs={{0,1},{1,2},{2,3},{4,5},{5,6},{6,7},{8,9},{9,10},{10,11},{12,13},{... | collective-permute-start | bytes 49160 | tf_op jit(solution)/shard_map/ppermute | solution.py:71
  8.7 1.5 reshape.70.wd_ref
  10.2 2.2 collective-permute-done.1
  15.1 3.5 %collective-permute-done.3 = bf16[1,66,256]{2,1,0:T(8,128)(2,1)S(1)} collective-permute-done((bf16[1,66,256]{2,1,0:T(8,128)(2,1)S(1)}, bf16[1,66,256]{2,1,0:T(8,128)(2,1)S(1)}, u32[]{:S(2)}, u32[]{:S(2)}) %collective-permute-start.3) | collective-permute-done | bytes 33824 | tf_op jit(solution)/shard_map/ppermute | solution.py:71
  18.6 2.5 maximum_maximum_fusion
  21.1 34.2 %conv_forward.1 = (bf16[34,80,1024]{2,1,0:T(8,128)(2,1)}, bf16[2048,1024]{1,0:T(8,128)(2,1)}, bf16[2048,1024]{1,0:T(8,128)(2,1)}, bf16[2048,1024]{1,0:T(8,128)(2,1)}, bf16[2048,256]{1,0:T(8,128)(2,1)}) custom-call(bf16[2448,256]{1,0:T(8,128)(2,1)} %bitcast.35, bf16[2048,256]{1,0:T(8,128)(2,1)} %bitcast.31, f32[1,256]{1,0:T(1,128)} %bitcast.41, ...), custom_call_target="tpu_custom_call" | custom-call | tf_op jit(solution)/shard_map/conv_forward/pallas_call | solution.py:150
  58.3 7.1 %all-to-all-start = ((bf16[32,8,8,256]{3,2,1,0:T(8,128)(2,1)}), bf16[32,8,8,256]{3,2,1,0:T(8,128)(2,1)S(1)}, u32[]{:S(2)}, u32[]{:S(2)}) async-start(bf16[32,8,8,256]{3,2,1,0:T(8,128)(2,1)} %reshape.71), calls=%async_computation | async-start | bytes 2097152 | tf_op jit(solution)/shard_map/all_to_all | solution.py:465
  66.5 1.8 copy.80
  69.4 21.0 %all-to-all-done.mid_ref = bf16[32,8,8,256]{3,2,1,0:T(8,128)(2,1)S(1)} async-done(((bf16[32,8,8,256]{3,2,1,0:T(8,128)(2,1)}), bf16[32,8,8,256]{3,2,1,0:T(8,128)(2,1)S(1)}, u32[]{:S(2)}, u32[]{:S(2)}) %all-to-all-start) | async-done | bytes 1048608 | tf_op jit(solution)/shard_map/all_to_all | solution.py:465
  90.4 4.5 %all-to-all-start.1 = ((bf16[32,8,8,256]{3,2,1,0:T(8,128)(2,1)}), bf16[32,8,8,256]{3,2,1,0:T(8,128)(2,1)S(1)}, u32[]{:S(2)}, u32[]{:S(2)}) async-start(bf16[32,8,8,256]{3,2,1,0:T(8,128)(2,1)} %reshape.73), calls=%async_computation.1 | async-start | bytes 2097152 | tf_op jit(solution)/shard_map/all_to_all | solution.py:465
  96.7 23.3 %all-to-all-done.1.cot_ref = bf16[32,8,8,256]{3,2,1,0:T(8,128)(2,1)S(1)} async-done(((bf16[32,8,8,256]{3,2,1,0:T(8,128)(2,1)}), bf16[32,8,8,256]{3,2,1,0:T(8,128)(2,1)S(1)}, u32[]{:S(2)}, u32[]{:S(2)}) %all-to-all-start.1) | async-done | bytes 1048608 | tf_op jit(solution)/shard_map/all_to_all | solution.py:465
  120.9 47.1 %grid_attention.1 = (bf16[32,8,8,256]{3,2,1,0:T(8,128)(2,1)}, f32[768,256]{1,0:T(8,128)}, f32[256,256]{1,0:T(8,128)}, f32[256,1]{1,0:T(8,128)}) custom-call(bf16[32,8,8,256]{3,2,1,0:T(8,128)(2,1)} %copy-done.2, bf16[32,8,8,256]{3,2,1,0:T(8,128)(2,1)} %copy-done.3, f32[256,1]{1,0:T(8,128)} %copy.70.gain_ref, bf16[256,768]{1,0:T(8,128)(2,1)} %wq_ref.1, ...), custom_call_target="tpu_custom_call" | custom-call | tf_op jit(solution)/shard_map/grid_attention/pallas_call | solution.py:410
  168.0 4.8 %all-to-all-start.2 = ((bf16[32,8,8,256]{3,2,1,0:T(8,128)(2,1)}), bf16[32,8,8,256]{3,2,1,0:T(8,128)(2,1)}, u32[]{:S(2)}, u32[]{:S(2)}) async-start(bf16[32,8,8,256]{3,2,1,0:T(8,128)(2,1)} %get-tuple-element.32), calls=%async_computation.2 | async-start | bytes 2097152 | tf_op jit(solution)/shard_map/all_to_all | solution.py:482
  173.0 1.8 copy.72
  174.9 22.8 %all-to-all-done.2 = bf16[32,8,8,256]{3,2,1,0:T(8,128)(2,1)} async-done(((bf16[32,8,8,256]{3,2,1,0:T(8,128)(2,1)}), bf16[32,8,8,256]{3,2,1,0:T(8,128)(2,1)}, u32[]{:S(2)}, u32[]{:S(2)}) %all-to-all-start.2) | async-done | bytes 1048608 | tf_op jit(solution)/shard_map/all_to_all | solution.py:482
  197.7 1.6 reshape.82
  199.2 2.1 copy.79
  201.4 2.0 reshape.81
  203.4 1.9 copy.73
  205.2 2.6 fusion
  209.1 6.2 %conv_grad.1.gc_ref = bf16[2048,1024]{1,0:T(8,128)(2,1)} custom-call(bf16[2048,256]{1,0:T(8,128)(2,1)} %copy.74.gm_ref, bf16[1024,256]{1,0:T(8,128)(2,1)} %wp_ref.3, bf16[2048,1024]{1,0:T(8,128)(2,1)} %get-tuple-element.33.slope_ref), custom_call_target="tpu_custom_call" | custom-call | tf_op jit(solution)/shard_map/conv_grad/pallas_call | solution.py:195
  215.4 1.4 fusion.1
  216.8 5.0 %collective-permute-start.4 = (bf16[32,1,1024]{2,1,0:T(2,128)(2,1)S(1)}, bf16[32,1,1024]{2,1,0:T(2,128)(2,1)S(1)}, u32[]{:S(2)}, u32[]{:S(2)}) collective-permute-start(bf16[32,1,1024]{2,1,0:T(2,128)(2,1)S(1)} %get-tuple-element.54), channel_id=1, source_target_pairs={{0,1},{1,2},{2,3},{4,5},{5,6},{6,7},{8,9},{9,10},{10,11},{12,13},{... | collective-permute-start | bytes 196616 | tf_op jit(solution)/shard_map/ppermute | solution.py:71
  224.3 5.3 %collective-permute-done.5 = bf16[32,1,1024]{2,1,0:T(2,128)(2,1)S(1)} collective-permute-done((bf16[32,1,1024]{2,1,0:T(2,128)(2,1)S(1)}, bf16[32,1,1024]{2,1,0:T(2,128)(2,1)S(1)}, u32[]{:S(2)}, u32[]{:S(2)}) %collective-permute-start.5) | collective-permute-done | bytes 65568 | tf_op jit(solution)/shard_map/ppermute | solution.py:71
  232.6 15.1 %conv_weight_grads.1 = (f32[9,1024]{1,0:T(8,128)}, f32[1024,256]{1,0:T(8,128)}) custom-call(bf16[34,80,1024]{2,1,0:T(8,128)(2,1)} %get-tuple-element.37.hid_in, bf16[2048,1024]{1,0:T(8,128)(2,1)} %get-tuple-element.38.act_ref, bf16[2048,1024]{1,0:T(8,128)(2,1)} %conv_grad.1.gc_ref, bf16[256,2048]{1,0:T(8,128)(2,1)} %bitcast.33), custom_call_target="tpu_custom_call" | custom-call | flops 1111490560 | bytes 33554432 | tf_op jit(solution)/shard_map/conv_weight_grads/pallas_call | solution.py:237
  248.5 1.9 copy.75.gm_ref
  251.3 1.8 pad_maximum_fusion.side_ref
  253.0 23.8 %conv_back.1 = (f32[1024,256]{1,0:T(8,128)}, f32[1,256]{1,0:T(1,128)}, bf16[2048,256]{1,0:T(8,128)(2,1)}) custom-call(bf16[2048,1024]{1,0:T(8,128)(2,1)} %conv_grad.1.gc_ref, bf16[2,64,1024]{2,1,0:T(8,128)(2,1)} %pad_maximum_fusion.1.line_ref, bf16[34,16,1024]{2,1,0:T(8,128)(2,1)} %pad_maximum_fusion.side_ref, ...), custom_call_target="tpu_custom_call" | custom-call | tf_op jit(solution)/shard_map/conv_back/pallas_call | solution.py:320
  278.2 49.3 %sum_over_devices.1 = (f32[256,1024]{1,0:T(8,128)}, f32[1024,256]{1,0:T(8,128)}, f32[256,768]{1,0:T(8,128)}, f32[256,256]{1,0:T(8,128)}, f32[40,256]{1,0:T(8,128)}) custom-call(f32[1024,256]{1,0:T(8,128)} %get-tuple-element.36.ex_ref, f32[1024,256]{1,0:T(8,128)} %get-tuple-element.39.pr_ref, f32[768,256]{1,0:T(8,128)} %get-tuple-element.40.qk_ref, ...), custom_call_target="tpu_custom_call" | custom-call | tf_op jit(solution)/shard_map/sum_over_devices/pallas_call | solution.py:644
  327.6 1.4 fusion.8
  329.0 1.4 reshape.79
  330.4 2.3 copy.86
  (71 shorter events, 26.4 us)
Async XLA Ops:
  1.7 8.6 %collective-permute-start = (bf16[32,1,256]{2,1,0:T(2,128)(2,1)S(1)}, bf16[32,1,256]{2,1,0:T(2,128)(2,1)S(1)}, u32[]{:S(2)}, u32[]{:S(2)}) collective-permute-start(bf16[32,1,256]{2,1,0:T(2,128)(2,1)S(1)} %get-tuple-element.58), channel_id=1, source_target_pairs={{0,1},{1,2},{2,3},{4,5},{5,6},{6,7},{8,9},{9,10},{10,11},{12,13},{... | collective-permute-start | bytes 49160 | tf_op jit(solution)/shard_map/ppermute | solution.py:71
  6.6 5.8 %collective-permute-start.1 = (bf16[32,1,256]{2,1,0:T(2,128)(2,1)S(1)}, bf16[32,1,256]{2,1,0:T(2,128)(2,1)S(1)}, u32[]{:S(2)}, u32[]{:S(2)}) collective-permute-start(bf16[32,1,256]{2,1,0:T(2,128)(2,1)S(1)} %get-tuple-element.59), channel_id=1, source_target_pairs={{1,0},{2,1},{3,2},{5,4},{6,5},{7,6},{9,8},{10,9},{11,10},{13,12},{... | collective-permute-start | bytes 49160 | tf_op jit(solution)/shard_map/ppermute | solution.py:71
  12.4 2.6 collective-permute-start.2
  13.8 4.8 %collective-permute-start.3 = (bf16[1,66,256]{2,1,0:T(8,128)(2,1)S(1)}, bf16[1,66,256]{2,1,0:T(8,128)(2,1)S(1)}, u32[]{:S(2)}, u32[]{:S(2)}) collective-permute-start(bf16[1,66,256]{2,1,0:T(8,128)(2,1)S(1)} %pad_maximum_fusion.5), channel_id=1, source_target_pairs={{4,0},{8,4},{12,8},{16,12},{20,16},{24,20},{28,24},{5,1},{9,5},{13... | collective-permute-start | bytes 101384 | tf_op jit(solution)/shard_map/ppermute | solution.py:71
  57.2 8.2 %copy-start.1 = (bf16[32,64,256]{2,1,0:T(8,128)(2,1)S(1)}, bf16[32,64,256]{2,1,0:T(8,128)(2,1)}, u32[]{:S(2)}) copy-start(bf16[32,64,256]{2,1,0:T(8,128)(2,1)} %param.10) | copy-start | bytes 3145732
  58.3 32.1 %all-to-all-start = ((bf16[32,8,8,256]{3,2,1,0:T(8,128)(2,1)}), bf16[32,8,8,256]{3,2,1,0:T(8,128)(2,1)S(1)}, u32[]{:S(2)}, u32[]{:S(2)}) async-start(bf16[32,8,8,256]{3,2,1,0:T(8,128)(2,1)} %reshape.71), calls=%async_computation | async-start | bytes 2097152 | tf_op jit(solution)/shard_map/all_to_all | solution.py:465
  68.3 26.6 %copy-start.4 = (bf16[256,768]{1,0:T(8,128)(2,1)S(1)}, bf16[256,768]{1,0:T(8,128)(2,1)}, u32[]{:S(2)}) copy-start(bf16[256,768]{1,0:T(8,128)(2,1)} %wq_ref.1) | copy-start | bytes 1179652
  68.3 27.6 %copy-start.9 = (f32[256]{0:T(256)S(1)}, f32[256]{0:T(256)}, u32[]{:S(2)}) copy-start(f32[256]{0:T(256)} %param.15) | copy-start | bytes 3076
  90.4 29.5 %copy-start.2 = (bf16[32,8,8,256]{3,2,1,0:T(8,128)(2,1)}, bf16[32,8,8,256]{3,2,1,0:T(8,128)(2,1)S(1)}, u32[]{:S(2)}) copy-start(bf16[32,8,8,256]{3,2,1,0:T(8,128)(2,1)S(1)} %all-to-all-done.mid_ref) | copy-start | bytes 3145732
  90.4 29.5 %all-to-all-start.1 = ((bf16[32,8,8,256]{3,2,1,0:T(8,128)(2,1)}), bf16[32,8,8,256]{3,2,1,0:T(8,128)(2,1)S(1)}, u32[]{:S(2)}, u32[]{:S(2)}) async-start(bf16[32,8,8,256]{3,2,1,0:T(8,128)(2,1)} %reshape.73), calls=%async_computation.1 | async-start | bytes 2097152 | tf_op jit(solution)/shard_map/all_to_all | solution.py:465
  120.0 1.0 copy-start.3
  168.0 29.6 %all-to-all-start.2 = ((bf16[32,8,8,256]{3,2,1,0:T(8,128)(2,1)}), bf16[32,8,8,256]{3,2,1,0:T(8,128)(2,1)}, u32[]{:S(2)}, u32[]{:S(2)}) async-start(bf16[32,8,8,256]{3,2,1,0:T(8,128)(2,1)} %get-tuple-element.32), calls=%async_computation.2 | async-start | bytes 2097152 | tf_op jit(solution)/shard_map/all_to_all | solution.py:482
  207.8 7.6 %copy-start = (bf16[2048,256]{0,1:T(8,128)(2,1)}, bf16[2048,256]{0,1:T(8,128)(2,1)S(1)}, u32[]{:S(2)}) copy-start(bf16[2048,256]{0,1:T(8,128)(2,1)S(1)} %get-tuple-element.50) | copy-start | bytes 3145732
  209.1 23.3 %copy-start.8 = (f32[256,1]{1,0:T(8,128)S(1)}, f32[256,1]{1,0:T(8,128)}, u32[]{:S(2)}) copy-start(f32[256,1]{1,0:T(8,128)} %get-tuple-element.44) | copy-start | bytes 3076
  216.8 7.5 %collective-permute-start.4 = (bf16[32,1,1024]{2,1,0:T(2,128)(2,1)S(1)}, bf16[32,1,1024]{2,1,0:T(2,128)(2,1)S(1)}, u32[]{:S(2)}, u32[]{:S(2)}) collective-permute-start(bf16[32,1,1024]{2,1,0:T(2,128)(2,1)S(1)} %get-tuple-element.54), channel_id=1, source_target_pairs={{0,1},{1,2},{2,3},{4,5},{5,6},{6,7},{8,9},{9,10},{10,11},{12,13},{... | collective-permute-start | bytes 196616 | tf_op jit(solution)/shard_map/ppermute | solution.py:71
  222.8 6.9 %collective-permute-start.5 = (bf16[32,1,1024]{2,1,0:T(2,128)(2,1)S(1)}, bf16[32,1,1024]{2,1,0:T(2,128)(2,1)S(1)}, u32[]{:S(2)}, u32[]{:S(2)}) collective-permute-start(bf16[32,1,1024]{2,1,0:T(2,128)(2,1)S(1)} %get-tuple-element.55), channel_id=1, source_target_pairs={{1,0},{2,1},{3,2},{5,4},{6,5},{7,6},{9,8},{10,9},{11,10},{13,12},{... | collective-permute-start | bytes 196616 | tf_op jit(solution)/shard_map/ppermute | solution.py:71
  229.7 20.7 %collective-permute-start.6 = (bf16[1,66,1024]{2,1,0:T(8,128)(2,1)S(1)}, bf16[1,66,1024]{2,1,0:T(8,128)(2,1)S(1)}, u32[]{:S(2)}, u32[]{:S(2)}) collective-permute-start(bf16[1,66,1024]{2,1,0:T(8,128)(2,1)S(1)} %pad_maximum_fusion.2), channel_id=1, source_target_pairs={{0,4},{4,8},{8,12},{12,16},{16,20},{20,24},{24,28},{1,5},{5,9},{9,... | collective-permute-start | bytes 405512 | tf_op jit(solution)/shard_map/ppermute | solution.py:71
  231.1 19.3 %collective-permute-start.7 = (bf16[1,66,1024]{2,1,0:T(8,128)(2,1)S(1)}, bf16[1,66,1024]{2,1,0:T(8,128)(2,1)S(1)}, u32[]{:S(2)}, u32[]{:S(2)}) collective-permute-start(bf16[1,66,1024]{2,1,0:T(8,128)(2,1)S(1)} %pad_maximum_fusion.3), channel_id=1, source_target_pairs={{4,0},{8,4},{12,8},{16,12},{20,16},{24,20},{28,24},{5,1},{9,5},{13... | collective-permute-start | bytes 405512 | tf_op jit(solution)/shard_map/ppermute | solution.py:71
  327.6 5.2 %copy-start.5 = (f32[1024,256]{1,0:T(8,128)S(1)}, f32[1024,256]{1,0:T(8,128)}, u32[]{:S(2)}) copy-start(f32[1024,256]{1,0:T(8,128)} %get-tuple-element.90) | copy-start | bytes 3145732
  327.6 6.1 %copy-start.6 = (f32[256,768]{1,0:T(8,128)S(1)}, f32[256,768]{1,0:T(8,128)}, u32[]{:S(2)}) copy-start(f32[256,768]{1,0:T(8,128)} %get-tuple-element.92) | copy-start | bytes 2359300
  332.7 1.9 copy-start.7

commit v3 on v2

--- a/solution.py
+++ b/solution.py
@@ -17,6 +17,7 @@
 F32 = jnp.float32
 BF16 = jnp.bfloat16
 EDGE = 8
+log2_e = 1.4426950408889634
 BLOCK_E = 256
 VMEM_BYTES = 56 * 1024 * 1024
 
@@ -60,6 +61,10 @@
     )
 
 
+def cost(micros):
+    return pl.CostEstimate(flops=int(micros * 1.1e9), bytes_accessed=1 << 20, transcendentals=0)
+
+
 def full(shape):
     return pl.BlockSpec(shape, lambda step: (0,) * len(shape))
 
@@ -76,11 +81,12 @@
     right = shift("col", block[:, :1], False)
     wide_last = jnp.concatenate([left[-1:], block[-1:], right[-1:]], axis=1)
     wide_first = jnp.concatenate([left[:1], block[:1], right[:1]], axis=1)
+    first = left
     above = shift("row", wide_last, True)
     below = shift("row", wide_first, False)
     left = jnp.concatenate([above[:, :1], left, below[:, :1]], axis=0)
     right = jnp.concatenate([above[:, -1:], right, below[:, -1:]], axis=0)
-    return above[:, 1:-1], below[:, 1:-1], left, right
+    return above[:, 1:-1], below[:, 1:-1], left, right, first
 
 
 def conv_forward(ext, core, gain, w_expand, w_taps, w_project, rows, cols):
@@ -179,15 +185,24 @@
             pltpu.VMEM((cells, chans), F32),
         ],
         compiler_params=params(),
+        cost_estimate=cost(34),
         name="conv_forward",
     )(ext, core, gain, w_expand, w_taps, w_project)
 
 
-def conv_grad(grad_mid_b, w_project, slope):
-    cells, chans = grad_mid_b.shape
+def conv_grad(cotangent, branch, w_project, slope):
+    cells, chans = cotangent.shape
     expand_w = w_project.shape[0]
 
-    def kernel(gm_ref, wp_ref, slope_ref, out_ref):
+    def kernel(cot_ref, branch_ref, wp_ref, slope_ref, out_ref, mid_out, mid_t_out, gm_ref):
+        @pl.when(pl.program_id(0) == 0)
+        def _():
+            grad_mid = cot_ref[...].astype(F32) + branch_ref[...].astype(F32)
+            mid_out[...] = grad_mid
+            rounded = grad_mid.astype(BF16)
+            gm_ref[...] = rounded
+            mid_t_out[...] = rounded.T
+
         grad_acted = dot_nt(gm_ref[...], wp_ref[...]).astype(BF16).astype(F32)
         out_ref[...] = (grad_acted * slope_ref[...].astype(F32)).astype(BF16)
 
@@ -197,23 +212,50 @@
         grid=(expand_w // BLOCK_E,),
         in_specs=[
             full((cells, chans)),
+            full((cells, chans)),
             pl.BlockSpec((BLOCK_E, chans), lambda step: (step, 0)),
             by_cell,
         ],
-        out_specs=by_cell,
-        out_shape=jax.ShapeDtypeStruct((cells, expand_w), BF16),
+        out_specs=[by_cell, full((cells, chans)), full((chans, cells))],
+        out_shape=[
+            jax.ShapeDtypeStruct((cells, expand_w), BF16),
+            jax.ShapeDtypeStruct((cells, chans), F32),
+            jax.ShapeDtypeStruct((chans, cells), BF16),
+        ],
+        scratch_shapes=[pltpu.VMEM((cells, chans), BF16)],
         compiler_params=params(),
+        cost_estimate=cost(8),
         name="conv_grad",
-    )(grad_mid_b, w_project, slope)
-
-
-def conv_weight_grads(hidden, acted, grad_conv, grad_mid_t, rows, cols):
+    )(cotangent, branch, w_project, slope)
+
+
+def project_grad(acted, grad_mid_t):
     cells, expand_w = acted.shape
     chans = grad_mid_t.shape[0]
+
+    def kernel(act_ref, gmt_ref, proj_out):
+        proj_out[...] = dot_nn(gmt_ref[...], act_ref[...])
+
+    return pl.pallas_call(
+        kernel,
+        grid=(expand_w // BLOCK_E,),
+        in_specs=[
+            pl.BlockSpec((cells, BLOCK_E), lambda step: (0, step)),
+            full((chans, cells)),
+        ],
+        out_specs=pl.BlockSpec((chans, BLOCK_E), lambda step: (step, 0)),
+        out_shape=jax.ShapeDtypeStruct((expand_w // BLOCK_E * chans, BLOCK_E), F32),
+        compiler_params=params(),
+        cost_estimate=cost(4),
+        name="project_grad",
+    )(acted, grad_mid_t)
+
+
+def depth_grad(hidden, grad_conv, rows, cols):
+    cells, expand_w = grad_conv.shape
     wide = hidden.shape[1]
 
-    def kernel(hid_in, act_ref, gc_ref, gmt_ref, depth_out, proj_out, hid_ref):
-        proj_out[...] = dot_nn(gmt_ref[...], act_ref[...])
+    def kernel(hid_in, gc_ref, depth_out, hid_ref):
         hid_ref[...] = hid_in[...].astype(F32)
 
         def one_row(index, carry):
@@ -240,24 +282,14 @@
         in_specs=[
             pl.BlockSpec((rows + 2, wide, BLOCK_E), lambda step: (0, 0, step)),
             by_cell,
-            by_cell,
-            full((chans, cells)),
-        ],
-        out_specs=[
-            pl.BlockSpec((9, BLOCK_E), lambda step: (0, step)),
-            pl.BlockSpec((chans, BLOCK_E), lambda step: (step, 0)),
-        ],
-        out_shape=[
-            jax.ShapeDtypeStruct((9, expand_w), F32),
-            jax.ShapeDtypeStruct((expand_w // BLOCK_E * chans, BLOCK_E), F32),
-        ],
+        ],
+        out_specs=pl.BlockSpec((9, BLOCK_E), lambda step: (0, step)),
+        out_shape=jax.ShapeDtypeStruct((9, expand_w), F32),
         scratch_shapes=[pltpu.VMEM((rows + 2, wide, BLOCK_E), F32)],
         compiler_params=params(),
-        cost_estimate=pl.CostEstimate(
-            flops=2 * cells * expand_w * (chans + 9), bytes_accessed=32 << 20, transcendentals=0
-        ),
-        name="conv_weight_grads",
-    )(hidden, acted, grad_conv, grad_mid_t)
+        cost_estimate=cost(12),
+        name="depth_grad",
+    )(hidden, grad_conv)
 
 
 def conv_back(grad_conv, line_pair, side_pair, slope, w_expand, w_taps, core, gain, grad_mid, rows, cols):
@@ -348,6 +380,7 @@
             pltpu.VMEM((cells, chans), F32),
         ],
         compiler_params=params(),
+        cost_estimate=cost(24),
         name="conv_back",
     )(grad_conv, line_pair, side_pair, slope, w_expand, w_taps, core, gain, grad_mid)
 
@@ -384,17 +417,17 @@
             at_v = slice(2 * chans + h * head, 2 * chans + (h + 1) * head)
             query, key, value = proj_ref[at_q], proj_ref[at_k], proj_ref[at_v]
             grad_att = gatt_ref[at_q]
-            scores = dot_tn(key, query) * scale
-            expons = jnp.exp(scores - jnp.max(scores, axis=0, keepdims=True))
+            scores = dot_tn(key, query)
+            expons = jnp.exp2((scores - jnp.max(scores, axis=0, keepdims=True)) * (scale * log2_e))
             probs = expons * (1.0 / jnp.sum(expons, axis=0, keepdims=True))
             probs_b = probs.astype(BF16)
             att_ref[at_q] = dot_nn(value, probs_b).astype(BF16)
             gproj_ref[at_v] = dot_nt(grad_att, probs_b).astype(BF16)
             grad_probs = dot_tn(value, grad_att)
             row_sum = jnp.sum(grad_probs * probs, axis=0, keepdims=True)
-            grad_scores = (scale * probs * (grad_probs - row_sum)).astype(BF16)
-            gproj_ref[at_q] = dot_nn(key, grad_scores).astype(BF16)
-            gproj_ref[at_k] = dot_nt(query, grad_scores).astype(BF16)
+            grad_scores = (probs * (grad_probs - row_sum)).astype(BF16)
+            gproj_ref[at_q] = (scale * dot_nn(key, grad_scores)).astype(BF16)
+            gproj_ref[at_k] = (scale * dot_nt(query, grad_scores)).astype(BF16)
         out_out[...] += dot_nn(att_ref[...], cot)
         qkv_out[...] += dot_nt(gproj_ref[...], scaled)
         grad_scaled = dot_nn(wq_ref[...], gproj_ref[...])
@@ -438,6 +471,7 @@
             pltpu.VMEM((chans, length), F32),
         ],
         compiler_params=params(),
+        cost_estimate=cost(45),
         name="grid_attention",
     )(mid_win, cot_win, gain_col, w_qkv, w_qkv_t, w_out)
 
@@ -466,7 +500,7 @@
 
     core = field_in.reshape(cells, chans)
     taps = w_depth.reshape(9, expand_w)
-    above, below, left, right = halo(field_in)
+    above, below, left, right, _ = halo(field_in)
     middle = jnp.concatenate([above, field_in, below], axis=0)
     gap = jnp.zeros((rows + 2, EDGE - 2, chans), BF16)
     ext = jnp.concatenate([middle, right, gap, left], axis=1).reshape(-1, chans)
@@ -479,18 +513,19 @@
     branch_win, grad_qkv_t, grad_out, grad_gain_attn = grid_attention(
         mid_win, cot_win, gain_attn.reshape(chans, 1), w_qkv, w_qkv.T, w_out
     )
+    grad_qkv_t, grad_out = lax.psum((grad_qkv_t, grad_out), ("row", "col"))
     moved = lax.all_to_all(branch_win, ("row", "col"), split_axis=0, concat_axis=0, tiled=True)
     moved = moved.reshape(
         row_devices, col_devices, part_rows, part_cols, per_row, per_col, chans
     )
     branch = moved.transpose(4, 0, 2, 5, 1, 3, 6).reshape(cells, chans)
-    grad_mid = cotangent.reshape(cells, chans).astype(F32) + branch.astype(F32)
-    grad_mid_b = grad_mid.astype(BF16)
-    grad_conv = conv_grad(grad_mid_b, w_project, slope_conv)
-    above, below, left, right = halo(grad_conv.reshape(rows, cols, expand_w))
-    grad_depth, grad_project_t = conv_weight_grads(
-        hidden, acted, grad_conv, grad_mid_b.T, rows, cols
-    )
+    grad_conv, grad_mid, grad_mid_t = conv_grad(
+        cotangent.reshape(cells, chans), branch, w_project, slope_conv
+    )
+    above, below, left, right, first = halo(grad_conv.reshape(rows, cols, expand_w))
+    grad_project_t = project_grad(acted, grad_mid_t)
+    held, _ = lax.optimization_barrier((hidden, first))
+    grad_depth = depth_grad(held, grad_conv, rows, cols)
     line_pair = jnp.concatenate([above, below], axis=0)
     gap = jnp.zeros((rows + 2, EDGE - 1, expand_w), BF16)
     side_pair = jnp.concatenate([gap, left, right, gap], axis=1)
@@ -507,8 +542,8 @@
             jnp.zeros((-(small_rows + 2) % 8, chans), F32),
         ]
     )
-    grad_expand, grad_project, grad_qkv, grad_out, small = sum_over_devices(
-        grad_expand, grad_project_t, grad_qkv_t, grad_out, small, grad_scale
+    grad_expand, grad_project, small = sum_over_devices(
+        grad_expand, grad_project_t, small, grad_scale
     )
     return (
         grad_field.reshape(rows, cols, chans),
@@ -517,16 +552,16 @@
         small[:small_rows].reshape(3, 3, expand_w),
         grad_project,
         small[small_rows + 1],
-        grad_qkv,
-        grad_out,
-    )
-
-
-def sum_over_devices(expand, project_t, qkv_t, out, small, grad_scale):
+        grad_qkv_t.T * grad_scale,
+        grad_out * grad_scale,
+    )
+
+
+def sum_over_devices(expand, project_t, small, grad_scale):
     lanes = 128
-    chans = out.shape[0]
-    halves = out.shape[1] // lanes
-    parts = (expand, project_t, qkv_t, out, small)
+    chans = expand.shape[1]
+    halves = chans // lanes
+    parts = (expand, project_t, small)
     starts = [0]
     for part in parts:
         starts.append(starts[-1] + part.shape[0])
@@ -541,8 +576,7 @@
     count = len(orders[0])
 
     def kernel(
-        ex_ref, pr_ref, qk_ref, ou_ref, sm_ref,
-        ex_out, pr_out, qk_out, ou_out, sm_out,
+        ex_ref, pr_ref, sm_ref, ex_out, pr_out, sm_out,
         acc_ref, send_ref, recv_ref, got_ref, send_sem, recv_sem,
     ):
         places = {"row": lax.axis_index("row"), "col": lax.axis_index("col")}
@@ -561,7 +595,7 @@
 
         for lane in range(halves):
             span = slice(lane * lanes, (lane + 1) * lanes)
-            for start, ref in zip(starts, (ex_ref, pr_ref, qk_ref, ou_ref, sm_ref)):
+            for start, ref in zip(starts, (ex_ref, pr_ref, sm_ref)):
                 acc_ref[lane, start : start + ref.shape[0]] = ref[:, span]
             if total > starts[-1]:
                 acc_ref[lane, starts[-1] : total] = jnp.zeros((total - starts[-1], lanes), F32)
@@ -633,14 +667,10 @@
             low, high = block * chans, (block + 1) * chans
             ex_out[:, low:high] = read(starts[0] + low, chans)
             pr_out[low:high] = read(starts[1] + low, chans).T
-        for block in range(qkv_t.shape[0] // chans):
-            low, high = block * chans, (block + 1) * chans
-            qk_out[:, low:high] = read(starts[2] + low, chans).T
-        ou_out[...] = read(starts[3], chans)
         packed = -(-small.shape[0] // 16) * 16
-        sm_out[...] = read(starts[4], packed)[: small.shape[0]]
-
-    whole = [pl.BlockSpec(memory_space=pltpu.VMEM)] * 5
+        sm_out[...] = read(starts[2], packed)[: small.shape[0]]
+
+    whole = [pl.BlockSpec(memory_space=pltpu.VMEM)] * 3
     return pl.pallas_call(
         kernel,
         in_specs=whole,
@@ -648,8 +678,6 @@
         out_shape=[
             jax.ShapeDtypeStruct((chans, blocks * chans), F32),
             jax.ShapeDtypeStruct((blocks * chans, chans), F32),
-            jax.ShapeDtypeStruct((chans, qkv_t.shape[0]), F32),
-            jax.ShapeDtypeStruct(out.shape, F32),
             jax.ShapeDtypeStruct(small.shape, F32),
         ],
         scratch_shapes=[

time: 336 us -> 446 us (1.33)
  waiting for transfers between devices: 78.4 us -> 191 us
  between operations: 0.99 us -> 14.4 us
  local copies, waits for them, and re-layouts: 36.9 us -> 23.7 us
    psum x0 -> x1, waiting for transfers between devices: none -> 139 us  [shards(): grad_qkv_t, grad_out = lax.psum((grad_qkv_t, grad_out), ('row', 'col'))]
    all_to_all x1, waiting for transfers between devices: 22.8 us -> 0.01 us  [shards(): lax.all_to_all(branch_win, ('row', 'col'), split_axis=0, concat_axis=0, t...]
    convert_element_type x6 -> x0, local copies, waits for them, and re-layouts: 10.7 us -> none  [the longest x5 9.37 us: shards(): grad_mid = cotangent.reshape(cells, chans).astype(F32) + branch.astype(F32)]
    ppermute x8, waiting for transfers between devices: 11.2 us -> 5.69 us  [shift(): return lax.ppermute(block, axis, pairs)]
    pallas_call x1 -> x2, Pallas kernels: 15.1 us -> 17.5 us  [the longest x1 12.3 us: depth_grad(): pl.pallas_call(kernel, grid=(expand_w // BLOCK_E,), in_specs=[pl.BlockSpe...]
  transfers between devices with their start and end apart: 11 -> 12, of which waited for: 7 -> 5; matrix products, arithmetic and copies ran while one was open for 4% -> 3% of each run, Pallas kernels for 4% -> 4%
where the time goes in v3:
time: 446 us; the launch traced here: 445 us
  waiting for transfers between devices  191 us (43%)
  Pallas kernels  175 us (39%)
  starting transfers between devices  32.2 us (7%)
  local copies, waits for them, and re-layouts  23.7 us (5%)
  between operations  14.4 us (3%)
  other arithmetic  8.47 us (2%)
    psum x1, waiting for transfers between devices, shards(): grad_qkv_t, grad_out = lax.psum((grad_qkv_t, grad_out), ('row', 'col'))  139 us
    all_to_all x2, waiting for transfers between devices, to_windows(): lax.all_to_all(arranged, ('row', 'col'), split_axis=0, concat_axis=0, til...  46.4 us
    pallas_call x1, Pallas kernels, grid_attention(): pl.pallas_call(kernel, grid=(windows,), in_specs=[by_window, by_window, f...  46.4 us
    pallas_call x1, Pallas kernels, sum_over_devices(): pl.pallas_call(kernel, in_specs=whole, out_specs=whole, out_shape=[jax.Sh...  45.4 us
    pallas_call x1, Pallas kernels, conv_forward(): pl.pallas_call(kernel, grid=(steps,), in_specs=[full((ext_cells, chans)),...  34.2 us
    pallas_call x1, Pallas kernels, conv_back(): pl.pallas_call(kernel, grid=(steps,), in_specs=[by_cell, pl.BlockSpec((2,...  23.8 us
    ppermute x8, starting transfers between devices, shift(): return lax.ppermute(block, axis, pairs)  16 us
    pallas_call x1, Pallas kernels, depth_grad(): pl.pallas_call(kernel, grid=(expand_w // BLOCK_E,), in_specs=[pl.BlockSpe...  12.3 us
  transfers between devices with their start and end apart: 12, of which 5 were waited for; matrix products, arithmetic and copies ran while one was open for 3% of the time, Pallas kernels for 4%

profile of v3, /device:TPU:0, one launch (start us, length us, event | category | flops | bytes accessed | tf_op | source)
XLA Modules:
  0.0 445.2 jit_solution(2211145253567474288)
XLA Ops:
  8.2 4.9 %collective-permute-start = (bf16[32,1,256]{2,1,0:T(2,128)(2,1)S(1)}, bf16[32,1,256]{2,1,0:T(2,128)(2,1)S(1)}, u32[]{:S(2)}, u32[]{:S(2)}) collective-permute-start(bf16[32,1,256]{2,1,0:T(2,128)(2,1)S(1)} %get-tuple-element.98), channel_id=1, source_target_pairs={{0,1},{1,2},{2,3},{4,5},{5,6},{6,7},{8,9},{9,10},{10,11},{12,13},{... | collective-permute-start | bytes 49160 | tf_op jit(solution)/shard_map/ppermute | solution.py:76
  13.1 1.3 collective-permute-start.1
  15.2 1.4 reshape.71.wd_ref
  16.8 2.2 collective-permute-done.1
  19.0 1.3 collective-permute-start.2
  20.3 1.3 collective-permute-start.3
  21.6 3.5 collective-permute-done.3
  25.1 2.4 maximum_maximum_fusion
  27.6 34.2 %conv_forward.1 = (bf16[34,80,1024]{2,1,0:T(8,128)(2,1)}, bf16[2048,1024]{1,0:T(8,128)(2,1)}, bf16[2048,1024]{1,0:T(8,128)(2,1)}, bf16[2048,1024]{1,0:T(8,128)(2,1)}, bf16[2048,256]{1,0:T(8,128)(2,1)}) custom-call(bf16[2448,256]{1,0:T(8,128)(2,1)} %bitcast.34, bf16[2048,256]{1,0:T(8,128)(2,1)} %bitcast.32, f32[1,256]{1,0:T(1,128)} %bitcast.43, ...), custom_call_target="tpu_custom_call" | custom-call | flops 37399998464 | bytes 1048576 | tf_op jit(solution)/shard_map/conv_forward/pallas_call | solution.py:156
  61.8 1.3 reshape_reshape.3
  64.8 7.1 %all-to-all-start = ((bf16[32,8,8,256]{3,2,1,0:T(8,128)(2,1)}), bf16[32,8,8,256]{3,2,1,0:T(8,128)(2,1)S(1)}, u32[]{:S(2)}, u32[]{:S(2)}) async-start(bf16[32,8,8,256]{3,2,1,0:T(8,128)(2,1)} %reshape.72), calls=%async_computation | async-start | bytes 2097152 | tf_op jit(solution)/shard_map/all_to_all | solution.py:499
  73.9 23.1 %all-to-all-done.mid_ref = bf16[32,8,8,256]{3,2,1,0:T(8,128)(2,1)S(1)} async-done(((bf16[32,8,8,256]{3,2,1,0:T(8,128)(2,1)}), bf16[32,8,8,256]{3,2,1,0:T(8,128)(2,1)S(1)}, u32[]{:S(2)}, u32[]{:S(2)}) %all-to-all-start) | async-done | bytes 1048608 | tf_op jit(solution)/shard_map/all_to_all | solution.py:499
  97.0 4.5 all-to-all-start.1
  103.2 23.3 %all-to-all-done.1.cot_ref = bf16[32,8,8,256]{3,2,1,0:T(8,128)(2,1)S(1)} async-done(((bf16[32,8,8,256]{3,2,1,0:T(8,128)(2,1)}), bf16[32,8,8,256]{3,2,1,0:T(8,128)(2,1)S(1)}, u32[]{:S(2)}, u32[]{:S(2)}) %all-to-all-start.1) | async-done | bytes 1048608 | tf_op jit(solution)/shard_map/all_to_all | solution.py:499
  127.5 46.4 %grid_attention.1 = (bf16[32,8,8,256]{3,2,1,0:T(8,128)(2,1)}, f32[768,256]{1,0:T(8,128)}, f32[256,256]{1,0:T(8,128)}, f32[256,1]{1,0:T(8,128)}) custom-call(bf16[32,8,8,256]{3,2,1,0:T(8,128)(2,1)} %copy-done.1, bf16[32,8,8,256]{3,2,1,0:T(8,128)(2,1)} %copy-done.2, f32[256,1]{1,0:T(8,128)} %copy.59.gain_ref, bf16[256,768]{1,0:T(8,128)(2,1)} %wq_ref.1, ...), custom_call_target="tpu_custom_call" | custom-call | flops 49500000256 | bytes 1048576 | tf_op jit(solution)/shard_map/grid_attention/pallas_call | solution.py:443
  173.8 4.5 %all-to-all-start.2 = ((bf16[32,8,8,256]{3,2,1,0:T(8,128)(2,1)}), bf16[32,8,8,256]{3,2,1,0:T(8,128)(2,1)S(1)}, u32[]{:S(2)}, u32[]{:S(2)}) async-start(bf16[32,8,8,256]{3,2,1,0:T(8,128)(2,1)} %get-tuple-element.32), calls=%async_computation.2 | async-start | bytes 2097152 | tf_op jit(solution)/shard_map/all_to_all | solution.py:517
  179.2 138.8 %all-reduce.3.cloned.1.call-done = (f32[768,256]{1,0:T(8,128)}, f32[256,256]{1,0:T(8,128)}) async-done(((f32[768,256]{1,0:T(8,128)}, f32[256,256]{1,0:T(8,128)}), (f32[768,256]{1,0:T(8,128)}, f32[256,256]{1,0:T(8,128)})) %all-reduce.3.cloned.1.call-update) | async-done | bytes 1048592 | tf_op jit(solution)/shard_map/psum | solution.py:516
  323.1 7.8 %conv_grad.1 = (bf16[2048,1024]{1,0:T(8,128)(2,1)}, f32[2048,256]{1,0:T(8,128)}, bf16[256,2048]{1,0:T(8,128)(2,1)}) custom-call(bf16[2048,256]{1,0:T(8,128)(2,1)} %bitcast.35, bf16[2048,256]{1,0:T(8,128)(2,1)} %reshape.77.branch_ref, bf16[1024,256]{1,0:T(8,128)(2,1)} %wp_ref.3, bf16[2048,1024]{1,0:T(8,128)(2,1)} %get-tuple-element.33.slope_ref), custom_call_target="tpu_custom_call" | custom-call | flops 8800000000 | bytes 1048576 | tf_op jit(solution)/shard_map/conv_grad/pallas_call | solution.py:210
  330.9 1.4 fusion
  332.3 3.3 collective-permute-start.4
  335.6 1.3 collective-permute-start.5
  336.9 5.2 %project_grad.1.pr_ref = f32[1024,256]{1,0:T(8,128)} custom-call(bf16[2048,1024]{1,0:T(8,128)(2,1)} %get-tuple-element.39.act_ref, bf16[256,2048]{1,0:T(8,128)(2,1)} %get-tuple-element.40.gmt_ref), custom_call_target="tpu_custom_call" | custom-call | flops 4400000000 | bytes 1048576 | tf_op jit(solution)/shard_map/project_grad/pallas_call | solution.py:239
  343.2 1.3 collective-permute-start.6
  344.6 1.3 collective-permute-start.7
  345.9 12.3 %depth_grad.1 = f32[9,1024]{1,0:T(8,128)} custom-call(bf16[34,80,1024]{2,1,0:T(8,128)(2,1)} %get-tuple-element.42.hid_in, bf16[2048,1024]{1,0:T(8,128)(2,1)} %get-tuple-element.34.gc_ref), custom_call_target="tpu_custom_call" | custom-call | flops 13200000000 | bytes 1048576 | tf_op jit(solution)/shard_map/depth_grad/pallas_call | solution.py:279
  360.0 1.7 pad_maximum_fusion.side_ref
  361.7 23.8 %conv_back.1 = (f32[1024,256]{1,0:T(8,128)}, f32[1,256]{1,0:T(1,128)}, bf16[2048,256]{1,0:T(8,128)(2,1)}) custom-call(bf16[2048,1024]{1,0:T(8,128)(2,1)} %get-tuple-element.34.gc_ref, bf16[2,64,1024]{2,1,0:T(8,128)(2,1)} %pad_maximum_fusion.1.line_ref, bf16[34,16,1024]{2,1,0:T(8,128)(2,1)} %pad_maximum_fusion.side_ref, ...), custom_call_target="tpu_custom_call" | custom-call | flops 26400000000 | bytes 1048576 | tf_op jit(solution)/shard_map/conv_back/pallas_call | solution.py:352
  385.6 1.4 maximum_maximum_fusion.1.sm_ref
  386.9 45.4 %sum_over_devices.1 = (f32[256,1024]{1,0:T(8,128)}, f32[1024,256]{1,0:T(8,128)}, f32[40,256]{1,0:T(8,128)}) custom-call(f32[1024,256]{1,0:T(8,128)} %get-tuple-element.38.ex_ref, f32[1024,256]{1,0:T(8,128)} %project_grad.1.pr_ref, f32[40,256]{1,0:T(8,128)} %maximum_maximum_fusion.1.sm_ref), custom_call_target="tpu_custom_call" | custom-call | tf_op jit(solution)/shard_map/sum_over_devices/pallas_call | solution.py:674
  432.3 1.4 fusion.7
  433.7 1.4 reshape.82
  435.1 2.3 copy.72
  (66 shorter events, 18.1 us)
Async XLA Ops:
  8.2 8.6 %collective-permute-start = (bf16[32,1,256]{2,1,0:T(2,128)(2,1)S(1)}, bf16[32,1,256]{2,1,0:T(2,128)(2,1)S(1)}, u32[]{:S(2)}, u32[]{:S(2)}) collective-permute-start(bf16[32,1,256]{2,1,0:T(2,128)(2,1)S(1)} %get-tuple-element.98), channel_id=1, source_target_pairs={{0,1},{1,2},{2,3},{4,5},{5,6},{6,7},{8,9},{9,10},{10,11},{12,13},{... | collective-permute-start | bytes 49160 | tf_op jit(solution)/shard_map/ppermute | solution.py:76
  13.1 5.8 %collective-permute-start.1 = (bf16[32,1,256]{2,1,0:T(2,128)(2,1)S(1)}, bf16[32,1,256]{2,1,0:T(2,128)(2,1)S(1)}, u32[]{:S(2)}, u32[]{:S(2)}) collective-permute-start(bf16[32,1,256]{2,1,0:T(2,128)(2,1)S(1)} %get-tuple-element.99), channel_id=1, source_target_pairs={{1,0},{2,1},{3,2},{5,4},{6,5},{7,6},{9,8},{10,9},{11,10},{13,12},{... | collective-permute-start | bytes 49160 | tf_op jit(solution)/shard_map/ppermute | solution.py:76
  19.0 2.6 collective-permute-start.2
  20.3 4.8 %collective-permute-start.3 = (bf16[1,66,256]{2,1,0:T(8,128)(2,1)S(1)}, bf16[1,66,256]{2,1,0:T(8,128)(2,1)S(1)}, u32[]{:S(2)}, u32[]{:S(2)}) collective-permute-start(bf16[1,66,256]{2,1,0:T(8,128)(2,1)S(1)} %pad_maximum_fusion.5), channel_id=1, source_target_pairs={{4,0},{8,4},{12,8},{16,12},{20,16},{24,20},{28,24},{5,1},{9,5},{13... | collective-permute-start | bytes 101384 | tf_op jit(solution)/shard_map/ppermute | solution.py:76
  63.7 8.2 %copy-start = (bf16[32,64,256]{2,1,0:T(8,128)(2,1)S(1)}, bf16[32,64,256]{2,1,0:T(8,128)(2,1)}, u32[]{:S(2)}) copy-start(bf16[32,64,256]{2,1,0:T(8,128)(2,1)} %param.10) | copy-start | bytes 3145732
  64.8 32.1 %all-to-all-start = ((bf16[32,8,8,256]{3,2,1,0:T(8,128)(2,1)}), bf16[32,8,8,256]{3,2,1,0:T(8,128)(2,1)S(1)}, u32[]{:S(2)}, u32[]{:S(2)}) async-start(bf16[32,8,8,256]{3,2,1,0:T(8,128)(2,1)} %reshape.72), calls=%async_computation | async-start | bytes 2097152 | tf_op jit(solution)/shard_map/all_to_all | solution.py:499
  72.8 28.7 %copy-start.4 = (bf16[256,768]{1,0:T(8,128)(2,1)S(1)}, bf16[256,768]{1,0:T(8,128)(2,1)}, u32[]{:S(2)}) copy-start(bf16[256,768]{1,0:T(8,128)(2,1)} %wq_ref.1) | copy-start | bytes 1179652
  72.8 29.6 %copy-start.7 = (f32[256]{0:T(256)S(1)}, f32[256]{0:T(256)}, u32[]{:S(2)}) copy-start(f32[256]{0:T(256)} %param.15) | copy-start | bytes 3076
  97.0 29.5 %copy-start.1 = (bf16[32,8,8,256]{3,2,1,0:T(8,128)(2,1)}, bf16[32,8,8,256]{3,2,1,0:T(8,128)(2,1)S(1)}, u32[]{:S(2)}) copy-start(bf16[32,8,8,256]{3,2,1,0:T(8,128)(2,1)S(1)} %all-to-all-done.mid_ref) | copy-start | bytes 3145732
  97.0 29.5 %all-to-all-start.1 = ((bf16[32,8,8,256]{3,2,1,0:T(8,128)(2,1)}), bf16[32,8,8,256]{3,2,1,0:T(8,128)(2,1)S(1)}, u32[]{:S(2)}, u32[]{:S(2)}) async-start(bf16[32,8,8,256]{3,2,1,0:T(8,128)(2,1)} %reshape.74), calls=%async_computation.1 | async-start | bytes 2097152 | tf_op jit(solution)/shard_map/all_to_all | solution.py:499
  126.5 1.0 copy-start.2
  173.8 5.3 %copy-start.6 = (f32[256,1]{1,0:T(8,128)S(1)}, f32[256,1]{1,0:T(8,128)}, u32[]{:S(2)}) copy-start(f32[256,1]{1,0:T(8,128)} %get-tuple-element.44) | copy-start | bytes 3076
  173.8 147.3 %all-to-all-start.2 = ((bf16[32,8,8,256]{3,2,1,0:T(8,128)(2,1)}), bf16[32,8,8,256]{3,2,1,0:T(8,128)(2,1)S(1)}, u32[]{:S(2)}, u32[]{:S(2)}) async-start(bf16[32,8,8,256]{3,2,1,0:T(8,128)(2,1)} %get-tuple-element.32), calls=%async_computation.2 | async-start | bytes 2097152 | tf_op jit(solution)/shard_map/all_to_all | solution.py:517
  178.3 139.7 %all-reduce.3.cloned.1.call-start = ((), (), s32[]{:S(2)}) async-start(), calls=%async_computation.3 | async-start | bytes 2097152 | tf_op jit(solution)/shard_map/psum | solution.py:516
  318.0 2.4 copy-start.5
  332.3 10.8 %collective-permute-start.4 = (bf16[32,1,1024]{2,1,0:T(2,128)(2,1)S(1)}, bf16[32,1,1024]{2,1,0:T(2,128)(2,1)S(1)}, u32[]{:S(2)}, u32[]{:S(2)}) collective-permute-start(bf16[32,1,1024]{2,1,0:T(2,128)(2,1)S(1)} %get-tuple-element.94), channel_id=1, source_target_pairs={{0,1},{1,2},{2,3},{4,5},{5,6},{6,7},{8,9},{9,10},{10,11},{12,13},{... | collective-permute-start | bytes 196616 | tf_op jit(solution)/shard_map/ppermute | solution.py:76
  335.6 7.5 %collective-permute-start.5 = (bf16[32,1,1024]{2,1,0:T(2,128)(2,1)S(1)}, bf16[32,1,1024]{2,1,0:T(2,128)(2,1)S(1)}, u32[]{:S(2)}, u32[]{:S(2)}) collective-permute-start(bf16[32,1,1024]{2,1,0:T(2,128)(2,1)S(1)} %get-tuple-element.95), channel_id=1, source_target_pairs={{1,0},{2,1},{3,2},{5,4},{6,5},{7,6},{9,8},{10,9},{11,10},{13,12},{... | collective-permute-start | bytes 196616 | tf_op jit(solution)/shard_map/ppermute | solution.py:76
  343.2 15.9 %collective-permute-start.6 = (bf16[1,66,1024]{2,1,0:T(8,128)(2,1)S(1)}, bf16[1,66,1024]{2,1,0:T(8,128)(2,1)S(1)}, u32[]{:S(2)}, u32[]{:S(2)}) collective-permute-start(bf16[1,66,1024]{2,1,0:T(8,128)(2,1)S(1)} %pad_maximum_fusion.2), channel_id=1, source_target_pairs={{0,4},{4,8},{8,12},{12,16},{16,20},{20,24},{24,28},{1,5},{5,9},{9,... | collective-permute-start | bytes 405512 | tf_op jit(solution)/shard_map/ppermute | solution.py:76
  344.6 14.5 %collective-permute-start.7 = (bf16[1,66,1024]{2,1,0:T(8,128)(2,1)S(1)}, bf16[1,66,1024]{2,1,0:T(8,128)(2,1)S(1)}, u32[]{:S(2)}, u32[]{:S(2)}) collective-permute-start(bf16[1,66,1024]{2,1,0:T(8,128)(2,1)S(1)} %pad_maximum_fusion.3), channel_id=1, source_target_pairs={{4,0},{8,4},{12,8},{16,12},{20,16},{24,20},{28,24},{5,1},{9,5},{13... | collective-permute-start | bytes 405512 | tf_op jit(solution)/shard_map/ppermute | solution.py:76
  432.3 5.1 %copy-start.3 = (f32[1024,256]{1,0:T(8,128)S(1)}, f32[1024,256]{1,0:T(8,128)}, u32[]{:S(2)}) copy-start(f32[1024,256]{1,0:T(8,128)} %get-tuple-element.130) | copy-start | bytes 3145732
Sparse Core Ops, SparseCore 0:
  185.1 132.8 all-reduce.2
